TPU v7x, 128 devices: a whole 4x4x4 slice. The times are simulated.
128 devices in a mesh: lvl: 8 (over y, core), clu: 16 (over z, x).
Axes of the slice: x: 4, y: 4, z: 4, core: 2. Of those that a mesh axis runs over, the one named last changes fastest.
Arguments:
- sources: bfloat16 [32, 2, 2097152], P(None, None, ('lvl', 'clu')), may hold values from -6 to 6
- source_order: int32 [128, 16384], P(('lvl', 'clu')), may hold values from 0 to 16383, each once within a row
- leaf_basis: bfloat16 [8192, 256, 128], P(('lvl', 'clu')), may hold values from -0.25 to 0.25
- leaf_ranks: int32 [8192], P(('lvl', 'clu')), may hold values from 16 to 64, as said below
- source_factors: bfloat16 [3, 8192, 2, 64, 128], P(None, ('lvl', 'clu')), may hold values from -0.375 to 0.375
- target_factors: bfloat16 [4, 8192, 2, 64, 128], P(None, ('lvl', 'clu')), may hold values from -0.375 to 0.375
- target_basis: bfloat16 [8192, 64, 512], P(('lvl', 'clu')), may hold values from -0.5 to 0.5
- target_order: int32 [128, 16384], P(('lvl', 'clu')), may hold values from 0 to 16383, each once within a row
Outputs:
- fields: bfloat16 [32, 2, 2097152], P(None, None, ('lvl', 'clu'))
Inputs may be any that keep to these rules, and one draw needn't show every extreme that they name: `leaf_ranks`: some leaf has rank 64.
All inputs are finite; a program needn't handle non-finite values.
Results may differ from a plain program's by a relative error of at most 0.019.
Values may be sent and summed in bfloat16 or wider, within the bound.
No kernel may reach another device: no remote copies, remote signals or barrier semaphores. Data moves between devices by JAX's collectives and lax.ppermute only.
A program may use at most 128 MiB of HBM per device.

v0:
```python
import functools

import jax
import jax.numpy as jnp
from jax import lax
from jax.experimental import pallas as pl
from jax.experimental.pallas import tpu as pltpu
from jax.sharding import PartitionSpec as P

F32 = jnp.float32
BF16 = jnp.bfloat16
LANES = 128
CUTS = ((0, 4),)


def lane_halves(shape):
    return lax.broadcasted_iota(jnp.int32, shape, 1) < shape[1] // 2


def packed_sum(first, second):
    turned = pltpu.roll(second, second.shape[1] // 2, 1)
    return first + jnp.where(lane_halves(first.shape), -turned, turned)


def sibling_rows(one, other):
    left = lane_halves(one.shape)
    half = one.shape[1] // 2
    real = jnp.where(left, one, pltpu.roll(other, half, 1))
    imag = jnp.where(left, pltpu.roll(one, half, 1), other)
    return jnp.concatenate([real, imag], axis=0)


def pairwise(steps, even, odd):
    def step(s, _):
        pl.when(s % 2 == 0)(functools.partial(even, s))
        pl.when(s % 2 == 1)(functools.partial(odd, s))
        return 0

    lax.fori_loop(0, steps, step, 0)


def fetch_order(order_ref, turned, order, order_sem):
    turned[...] = order_ref[...].T
    load = pltpu.make_async_copy(turned, order, order_sem)
    load.start()
    return load


def gather_rows(order, table, segment, held, base):
    for q in range(LANES):
        held[pl.ds(base + q, 1), :] = table[pl.ds(order.at[q][segment], 1), :]


def leaf_kernel(
    first, width, order_ref, ranks_ref, source_ref, basis_hbm, coef_ref,
    table, held0, held1, mixed, basis, turned, order, basis_sem, order_sem,
):
    rhs, _, count = source_ref.shape
    columns = 2 * rhs
    groups, _, points, packed = basis.shape
    segments = points // LANES
    per_group = 4
    load_basis = pltpu.make_async_copy(
        basis_hbm.at[:, pl.ds(first, width)], basis, basis_sem
    )
    load_basis.start()
    load_order = fetch_order(order_ref, turned, order, order_sem)

    def fill(k, _):
        block = pl.ds(pl.multiple_of(k * LANES, LANES), LANES)
        table[block, :columns] = source_ref[:, :, block].reshape(columns, LANES).T.astype(F32)
        return 0

    lax.fori_loop(0, count // LANES, fill, 0, unroll=8)
    load_order.wait()
    load_basis.wait()
    total = groups * width

    def collect(pair, held):
        for part in range(2):
            t = 2 * pair + part
            box = (t // width) * per_group + first + t % width
            for k in range(segments):
                gather_rows(order, table, segments * box + k, held.at[part], k * LANES)

    def project(pair, held):
        for part in range(2):
            t = 2 * pair + part
            group, place = t // width, t % width
            rows = held[part].astype(BF16)[:, :columns]
            mixed[part] = lax.dot_general(
                rows, basis[group, place], (((0,), (0,)), ((), ())), preferred_element_type=F32
            )
            out = packed_sum(
                mixed[part, pl.ds(0, rhs, 2), :], mixed[part, pl.ds(1, rhs, 2), :]
            )
            lane = lax.broadcasted_iota(jnp.int32, out.shape, 1) & (packed // 2 - 1)
            rank = ranks_ref[group * per_group + first + place]
            coef_ref[group, place] = jnp.where(lane < rank, out, 0.0).astype(BF16)

    def even(s):
        project(jnp.maximum(s - 1, 0), held1)
        collect(s, held0)

    def odd(s):
        project(s - 1, held0)
        collect(s, held1)

    pairwise(total // 2, even, odd)
    project(total // 2 - 1, held1)


def leaf_coefs(order, ranks, source, basis, first, width):
    rhs, _, count = source.shape
    groups, _, points, packed = basis.shape
    vmem = pl.BlockSpec(memory_space=pltpu.VMEM)
    smem = pl.BlockSpec(memory_space=pltpu.SMEM)
    hbm = pl.BlockSpec(memory_space=pl.ANY)
    return pl.pallas_call(
        functools.partial(leaf_kernel, first, width),
        out_shape=jax.ShapeDtypeStruct((groups, width, rhs, packed), BF16),
        in_specs=[vmem, smem, vmem, hbm],
        out_specs=vmem,
        scratch_shapes=[
            pltpu.VMEM((count, LANES), F32),
            pltpu.VMEM((2, points, LANES), F32),
            pltpu.VMEM((2, points, LANES), F32),
            pltpu.VMEM((2, 2 * rhs, packed), F32),
            pltpu.VMEM((groups, width, points, packed), BF16),
            pltpu.VMEM((LANES, count // LANES), jnp.int32),
            pltpu.SMEM((LANES, count // LANES), jnp.int32),
            pltpu.SemaphoreType.DMA,
            pltpu.SemaphoreType.DMA,
        ],
        compiler_params=pltpu.CompilerParams(vmem_limit_bytes=24 << 20),
        name="leaf_coefs",
    )(order, ranks, source, basis)


def mix_kernel(level, first, upper_ref, own_ref, other_ref, factor_ref, out_ref):
    groups, width = own_ref.shape[:2]
    upper = upper_ref[0]

    def step(t, _):
        group, place = t // width, t % width
        rows = sibling_rows(own_ref[group, place], other_ref[group, place])
        mine = factor_ref.at[level, group, first + place]
        factor = jnp.concatenate([mine[upper], mine[1 - upper]], axis=0)
        both = jnp.dot(rows, factor, preferred_element_type=F32)
        half = both.shape[0] // 2
        out_ref[group, place] = packed_sum(both[:half], both[half:]).astype(BF16)
        return 0

    lax.fori_loop(0, groups * width, step, 0, unroll=16)


def mix_level(upper, own, other, factors, level, first):
    vmem = pl.BlockSpec(memory_space=pltpu.VMEM)
    return pl.pallas_call(
        functools.partial(mix_kernel, level, first),
        out_shape=jax.ShapeDtypeStruct(own.shape, BF16),
        in_specs=[pl.BlockSpec(memory_space=pltpu.SMEM), vmem, vmem, vmem],
        out_specs=vmem,
        compiler_params=pltpu.CompilerParams(vmem_limit_bytes=16 << 20),
        name="mix_level",
    )(upper, own, other, factors)


def target_kernel(
    order_ref, coef_ref, factor_hbm, basis_hbm, out_ref,
    factor, basis, table, work0, work1, rows, held0, held1, turned, order,
    factor_sem, basis_sem, order_sem,
):
    levels, boxes = factor.shape[:2]
    rhs, packed = coef_ref.shape[1:]
    rank = packed // 2
    points = basis.shape[2] // 2
    columns = 2 * rhs
    blocks = order_ref.shape[0]
    loads = [
        pltpu.make_async_copy(factor_hbm.at[k], factor.at[k], factor_sem.at[k])
        for k in range(levels)
    ]
    loads.append(pltpu.make_async_copy(basis_hbm, basis, basis_sem))
    for load in loads:
        load.start()
    load_order = fetch_order(order_ref, turned, order, order_sem)
    low = 4
    source = coef_ref
    for k in range(levels):
        loads[k].wait()
        sink = (work0, work1)[k % 2]
        stride = low << k

        def pair(p, _, k=k, stride=stride, source=source, sink=sink):
            first = (p // stride) * (2 * stride) + p % stride
            second = first + stride
            lhs = sibling_rows(source[first], source[second])
            for box in (first, second):
                weights = factor[k, box].reshape(packed, packed)
                both = jnp.dot(lhs, weights, preferred_element_type=F32)
                sink[box] = packed_sum(both[:rhs], both[rhs:]).astype(BF16)
            return 0

        lax.fori_loop(0, boxes // 2, pair, 0, unroll=16)
        source = sink
    loads[levels].wait()

    def expand(box, _):
        coef = source[box].astype(F32)
        buf = rows.at[box % 8]
        buf[pl.ds(0, rhs, 2), :] = jnp.where(lane_halves(coef.shape), coef, -coef)
        buf[pl.ds(1, rhs, 2), :] = pltpu.roll(coef, rank, 1)
        weights = basis[box]
        weights = jnp.concatenate([weights[:, :points], weights[:, points:]], axis=0)
        field = jnp.dot(buf[...].astype(BF16), weights, preferred_element_type=F32).astype(BF16)
        spot = pl.ds(pl.multiple_of(box * points, points), points)
        table[spot, :columns] = field.T.astype(F32)
        return 0

    lax.fori_loop(0, boxes, expand, 0, unroll=8)
    load_order.wait()
    many = held0.shape[0]

    def collect(s, held):
        for part in range(many):
            gather_rows(order, table, many * s + part, held.at[part], 0)

    def place(s, held):
        for part in range(many):
            values = held[part].astype(BF16)[:, :columns].T
            spot = pl.ds(pl.multiple_of((many * s + part) * LANES, LANES), LANES)
            out_ref[:, :, spot] = values.reshape(rhs, 2, LANES)

    def even(s):
        place(jnp.maximum(s - 1, 0), held1)
        collect(s, held0)

    def odd(s):
        place(s - 1, held0)
        collect(s, held1)

    pairwise(blocks // many, even, odd)
    place(blocks // many - 1, held1)


def target_fields(order, coef, factors, basis):
    boxes, rhs, packed = coef.shape
    points = basis.shape[2] // 2
    count = boxes * points
    vmem = pl.BlockSpec(memory_space=pltpu.VMEM)
    hbm = pl.BlockSpec(memory_space=pl.ANY)
    return pl.pallas_call(
        target_kernel,
        out_shape=jax.ShapeDtypeStruct((rhs, 2, count), BF16),
        in_specs=[vmem, vmem, hbm, hbm],
        out_specs=vmem,
        scratch_shapes=[
            pltpu.VMEM(factors.shape, BF16),
            pltpu.VMEM(basis.shape, BF16),
            pltpu.VMEM((count, LANES), F32),
            pltpu.VMEM(coef.shape, BF16),
            pltpu.VMEM(coef.shape, BF16),
            pltpu.VMEM((8, 2 * rhs, packed), F32),
            pltpu.VMEM((4, LANES, LANES), F32),
            pltpu.VMEM((4, LANES, LANES), F32),
            pltpu.VMEM((LANES, count // LANES), jnp.int32),
            pltpu.SMEM((LANES, count // LANES), jnp.int32),
            pltpu.SemaphoreType.DMA((factors.shape[0],)),
            pltpu.SemaphoreType.DMA,
            pltpu.SemaphoreType.DMA,
        ],
        compiler_params=pltpu.CompilerParams(vmem_limit_bytes=36 << 20),
        name="target_fields",
    )(order, coef, factors, basis)


def local(
    sources,
    source_order,
    leaf_basis,
    leaf_ranks,
    source_factors,
    target_factors,
    target_basis,
    target_order,
):
    boxes, points, packed = leaf_basis.shape
    rhs, _, count = sources.shape
    groups = lax.axis_size("clu")
    per_group = boxes // groups
    order_in = source_order.reshape(count // LANES, LANES)
    order_out = target_order.reshape(count // LANES, LANES)
    basis = leaf_basis.reshape((groups, per_group) + leaf_basis.shape[1:])
    levels = source_factors.shape[0]
    factors = source_factors.reshape((levels, groups, per_group) + source_factors.shape[2:])
    size = lax.axis_size("lvl")
    uppers = [
        (lax.axis_index("lvl") >> level & 1).reshape(1).astype(jnp.int32)
        for level in range(levels)
    ]
    parts = []
    for first, width in CUTS:
        coef = leaf_coefs(order_in, leaf_ranks, sources, basis, first, width)
        for level in range(levels):
            other = lax.ppermute(coef, "lvl", [(i, i ^ 1 << level) for i in range(size)])
            coef = mix_level(uppers[level], coef, other, factors, level, first)
        parts.append(lax.all_to_all(coef, "clu", split_axis=0, concat_axis=0, tiled=True))
    coef = jnp.concatenate(parts, axis=1).reshape(boxes, rhs, packed)
    return target_fields(order_out, coef, target_factors, target_basis)


def solution(mesh):
    both = ("lvl", "clu")
    placed = (
        P(None, None, both),
        P(both, None),
        P(both, None, None),
        P(both),
        P(None, both, None, None, None),
        P(None, both, None, None, None),
        P(both, None, None),
        P(both, None),
    )
    return jax.shard_map(
        local, mesh=mesh, in_specs=placed, out_specs=P(None, None, both), check_vma=False
    )
```

profile of v0, /device:TPU:0, one launch (start us, length us, event | category | flops | bytes accessed | tf_op | source)
XLA Modules:
  0.0 112.9 jit_solution(1787951336570386988)
XLA Ops:
  0.0 0.0 copy-start.4
  0.0 2.2 %copy-done.4 = bf16[64,256,128]{2,1,0:T(8,128)(2,1)S(1)} copy-done((bf16[64,256,128]{2,1,0:T(8,128)(2,1)S(1)}, bf16[64,256,128]{2,1,0:T(8,128)(2,1)}, u32[]{:S(2)}) %copy-start.4) | copy-done | bytes 4194328
  2.2 0.0 copy-start.6
  2.2 1.6 %copy-done.6 = bf16[32,2,16384]{2,1,0:T(2,128)(2,1)S(1)} copy-done((bf16[32,2,16384]{2,1,0:T(2,128)(2,1)S(1)}, bf16[32,2,16384]{2,1,0:T(2,128)(2,1)}, u32[]{:S(2)}) %copy-start.6) | copy-done | bytes 2097176
  3.8 0.8 copy-done.7
  4.6 0.7 copy-done.9
  5.3 20.8 %leaf_coefs.1.own_ref = bf16[16,4,32,128]{3,2,1,0:T(8,128)(2,1)S(1)} custom-call(s32[128,128]{1,0:T(8,128)S(1)} %bitcast.13, s32[64]{0:T(128)S(1)} %copy-done.9, bf16[32,2,16384]{2,1,0:T(2,128)(2,1)S(1)} %copy-done.6, bf16[16,4,256,128]{3,2,1,0:T(8,128)(2,1)S(1)} %bitcast.11), custom_call_target="tpu_custom_call" | custom-call | tf_op jit(solution)/shard_map/leaf_coefs/pallas_call | solution.py:119
  26.1 0.1 collective-permute-start
  26.2 1.9 %collective-permute-done.other_ref = bf16[16,4,32,128]{3,2,1,0:T(8,128)(2,1)S(1)} collective-permute-done((bf16[16,4,32,128]{3,2,1,0:T(8,128)(2,1)S(1)}, bf16[16,4,32,128]{3,2,1,0:T(8,128)(2,1)S(1)}, u32[]{:S(2)}, u32[]{:S(2)}) %collective-permute-start) | collective-permute-done | bytes 524320 | tf_op jit(solution)/shard_map/ppermute | solution.py:306
  28.1 2.8 %copy-done = bf16[3,64,2,64,128]{4,3,2,1,0:T(8,128)(2,1)S(1)} copy-done((bf16[3,64,2,64,128]{4,3,2,1,0:T(8,128)(2,1)S(1)}, bf16[3,64,2,64,128]{4,3,2,1,0:T(8,128)(2,1)}, u32[]{:S(2)}) %copy-start) | copy-done | bytes 6291480
  30.9 1.7 %mix_level.3.own_ref = bf16[16,4,32,128]{3,2,1,0:T(8,128)(2,1)S(1)} custom-call(s32[1]{0:T(128)} %bitcast.3.upper_ref, bf16[16,4,32,128]{3,2,1,0:T(8,128)(2,1)S(1)} %leaf_coefs.1.own_ref, bf16[16,4,32,128]{3,2,1,0:T(8,128)(2,1)S(1)} %collective-permute-done.other_ref, bf16[3,16,4,2,64,128]{5,4,3,2,1,0:T(8,128)(2,1)S(1)} %bitcast.8), custom_call_target="tpu_custom_call" | custom-call | tf_op jit(solution)/shard_map/mix_level/pallas_call | solution.py:159
  32.5 1.7 %collective-permute-start.1 = (bf16[16,4,32,128]{3,2,1,0:T(8,128)(2,1)S(1)}, bf16[16,4,32,128]{3,2,1,0:T(8,128)(2,1)S(1)}, u32[]{:S(2)}, u32[]{:S(2)}) collective-permute-start(bf16[16,4,32,128]{3,2,1,0:T(8,128)(2,1)S(1)} %mix_level.3.own_ref), channel_id=1, source_target_pairs={{0,32},{16,48},{32,0},{48,16},{64,96},{80,112},{96,64},{112,80},{1... | collective-permute-start | bytes 1572872 | tf_op jit(solution)/shard_map/ppermute | solution.py:306
  34.3 12.3 %collective-permute-done.1.other_ref = bf16[16,4,32,128]{3,2,1,0:T(8,128)(2,1)S(1)} collective-permute-done((bf16[16,4,32,128]{3,2,1,0:T(8,128)(2,1)S(1)}, bf16[16,4,32,128]{3,2,1,0:T(8,128)(2,1)S(1)}, u32[]{:S(2)}, u32[]{:S(2)}) %collective-permute-start.1) | collective-permute-done | bytes 524320 | tf_op jit(solution)/shard_map/ppermute | solution.py:306
  46.6 2.8 %copy-done.1 = bf16[3,64,2,64,128]{4,3,2,1,0:T(8,128)(2,1)S(1)} copy-done((bf16[3,64,2,64,128]{4,3,2,1,0:T(8,128)(2,1)S(1)}, bf16[3,64,2,64,128]{4,3,2,1,0:T(8,128)(2,1)}, u32[]{:S(2)}) %copy-start.1) | copy-done | bytes 6291480
  49.4 1.7 %mix_level.4.own_ref = bf16[16,4,32,128]{3,2,1,0:T(8,128)(2,1)S(1)} custom-call(s32[1]{0:T(128)} %bitcast.2.upper_ref, bf16[16,4,32,128]{3,2,1,0:T(8,128)(2,1)S(1)} %mix_level.3.own_ref, bf16[16,4,32,128]{3,2,1,0:T(8,128)(2,1)S(1)} %collective-permute-done.1.other_ref, bf16[3,16,4,2,64,128]{5,4,3,2,1,0:T(8,128)(2,1)S(1)} %bitcast.9), custom_call_target="tpu_custom_call" | custom-call | tf_op jit(solution)/shard_map/mix_level/pallas_call | solution.py:159
  51.0 3.4 %collective-permute-start.2 = (bf16[16,4,32,128]{3,2,1,0:T(8,128)(2,1)S(1)}, bf16[16,4,32,128]{3,2,1,0:T(8,128)(2,1)S(1)}, u32[]{:S(2)}, u32[]{:S(2)}) collective-permute-start(bf16[16,4,32,128]{3,2,1,0:T(8,128)(2,1)S(1)} %mix_level.4.own_ref), channel_id=1, source_target_pairs={{0,64},{16,80},{32,96},{48,112},{64,0},{80,16},{96,32},{112,48},{1... | collective-permute-start | bytes 1572872 | tf_op jit(solution)/shard_map/ppermute | solution.py:306
  54.4 11.4 %collective-permute-done.2.other_ref = bf16[16,4,32,128]{3,2,1,0:T(8,128)(2,1)S(1)} collective-permute-done((bf16[16,4,32,128]{3,2,1,0:T(8,128)(2,1)S(1)}, bf16[16,4,32,128]{3,2,1,0:T(8,128)(2,1)S(1)}, u32[]{:S(2)}, u32[]{:S(2)}) %collective-permute-start.2) | collective-permute-done | bytes 524320 | tf_op jit(solution)/shard_map/ppermute | solution.py:306
  65.8 2.8 %copy-done.2 = bf16[3,64,2,64,128]{4,3,2,1,0:T(8,128)(2,1)S(1)} copy-done((bf16[3,64,2,64,128]{4,3,2,1,0:T(8,128)(2,1)S(1)}, bf16[3,64,2,64,128]{4,3,2,1,0:T(8,128)(2,1)}, u32[]{:S(2)}) %copy-start.2) | copy-done | bytes 6291480
  68.6 1.7 %mix_level.5 = bf16[16,4,32,128]{3,2,1,0:T(8,128)(2,1)S(1)} custom-call(s32[1]{0:T(128)} %bitcast.1.upper_ref, bf16[16,4,32,128]{3,2,1,0:T(8,128)(2,1)S(1)} %mix_level.4.own_ref, bf16[16,4,32,128]{3,2,1,0:T(8,128)(2,1)S(1)} %collective-permute-done.2.other_ref, bf16[3,16,4,2,64,128]{5,4,3,2,1,0:T(8,128)(2,1)S(1)} %bitcast.10), custom_call_target="tpu_custom_call" | custom-call | tf_op jit(solution)/shard_map/mix_level/pallas_call | solution.py:159
  70.2 17.8 %all_to_all.5 = bf16[16,4,32,128]{3,2,1,0:T(8,128)(2,1)S(1)} all-to-all(bf16[16,4,32,128]{3,2,1,0:T(8,128)(2,1)S(1)} %mix_level.5), channel_id=1, replica_groups=mesh['lvl'=8,'clu'=16] {'clu'}, dimensions={0} | all-to-all | bytes 1048576 | tf_op jit(solution)/shard_map/all_to_all | solution.py:308
  88.1 0.0 copy-done.5
  88.1 0.0 copy-done.8
  88.1 3.4 %copy-done.3 = bf16[4,64,2,64,128]{4,3,2,1,0:T(8,128)(2,1)S(1)} copy-done((bf16[4,64,2,64,128]{4,3,2,1,0:T(8,128)(2,1)S(1)}, bf16[4,64,2,64,128]{4,3,2,1,0:T(8,128)(2,1)}, u32[]{:S(2)}) %copy-start.3) | copy-done | bytes 8388632
  91.5 21.5 %target_fields.1 = bf16[32,2,16384]{2,1,0:T(2,128)(2,1)} custom-call(s32[128,128]{1,0:T(8,128)S(1)} %bitcast.14, bf16[64,32,128]{2,1,0:T(8,128)(2,1)S(1)} %bitcast.12, bf16[4,64,2,64,128]{4,3,2,1,0:T(8,128)(2,1)S(1)} %copy-done.3, bf16[64,64,512]{2,1,0:T(8,128)(2,1)S(1)} %copy-done.5), custom_call_target="tpu_custom_call" | custom-call | tf_op jit(solution)/shard_map/target_fields/pallas_call | solution.py:253
  (8 shorter events, 0.0 us)
Async XLA Ops:
  0.0 2.2 %copy-start.4 = (bf16[64,256,128]{2,1,0:T(8,128)(2,1)S(1)}, bf16[64,256,128]{2,1,0:T(8,128)(2,1)}, u32[]{:S(2)}) copy-start(bf16[64,256,128]{2,1,0:T(8,128)(2,1)} %param.10) | copy-start | bytes 12582916
  2.2 1.6 %copy-start.6 = (bf16[32,2,16384]{2,1,0:T(2,128)(2,1)S(1)}, bf16[32,2,16384]{2,1,0:T(2,128)(2,1)}, u32[]{:S(2)}) copy-start(bf16[32,2,16384]{2,1,0:T(2,128)(2,1)} %source_ref.1) | copy-start | bytes 6291460
  3.8 0.8 copy-start.7
  4.6 0.7 copy-start.9
  26.1 2.0 %collective-permute-start = (bf16[16,4,32,128]{3,2,1,0:T(8,128)(2,1)S(1)}, bf16[16,4,32,128]{3,2,1,0:T(8,128)(2,1)S(1)}, u32[]{:S(2)}, u32[]{:S(2)}) collective-permute-start(bf16[16,4,32,128]{3,2,1,0:T(8,128)(2,1)S(1)} %leaf_coefs.1.own_ref), channel_id=1, source_target_pairs={{0,16},{16,0},{32,48},{48,32},{64,80},{80,64},{96,112},{112,96},{1... | collective-permute-start | bytes 1572872 | tf_op jit(solution)/shard_map/ppermute | solution.py:306
  28.1 2.8 %copy-start = (bf16[3,64,2,64,128]{4,3,2,1,0:T(8,128)(2,1)S(1)}, bf16[3,64,2,64,128]{4,3,2,1,0:T(8,128)(2,1)}, u32[]{:S(2)}) copy-start(bf16[3,64,2,64,128]{4,3,2,1,0:T(8,128)(2,1)} %param.12) | copy-start | bytes 18874372
  32.5 14.0 %collective-permute-start.1 = (bf16[16,4,32,128]{3,2,1,0:T(8,128)(2,1)S(1)}, bf16[16,4,32,128]{3,2,1,0:T(8,128)(2,1)S(1)}, u32[]{:S(2)}, u32[]{:S(2)}) collective-permute-start(bf16[16,4,32,128]{3,2,1,0:T(8,128)(2,1)S(1)} %mix_level.3.own_ref), channel_id=1, source_target_pairs={{0,32},{16,48},{32,0},{48,16},{64,96},{80,112},{96,64},{112,80},{1... | collective-permute-start | bytes 1572872 | tf_op jit(solution)/shard_map/ppermute | solution.py:306
  46.6 2.8 %copy-start.1 = (bf16[3,64,2,64,128]{4,3,2,1,0:T(8,128)(2,1)S(1)}, bf16[3,64,2,64,128]{4,3,2,1,0:T(8,128)(2,1)}, u32[]{:S(2)}) copy-start(bf16[3,64,2,64,128]{4,3,2,1,0:T(8,128)(2,1)} %param.12) | copy-start | bytes 18874372
  51.0 14.7 %collective-permute-start.2 = (bf16[16,4,32,128]{3,2,1,0:T(8,128)(2,1)S(1)}, bf16[16,4,32,128]{3,2,1,0:T(8,128)(2,1)S(1)}, u32[]{:S(2)}, u32[]{:S(2)}) collective-permute-start(bf16[16,4,32,128]{3,2,1,0:T(8,128)(2,1)S(1)} %mix_level.4.own_ref), channel_id=1, source_target_pairs={{0,64},{16,80},{32,96},{48,112},{64,0},{80,16},{96,32},{112,48},{1... | collective-permute-start | bytes 1572872 | tf_op jit(solution)/shard_map/ppermute | solution.py:306
  65.8 2.8 %copy-start.2 = (bf16[3,64,2,64,128]{4,3,2,1,0:T(8,128)(2,1)S(1)}, bf16[3,64,2,64,128]{4,3,2,1,0:T(8,128)(2,1)}, u32[]{:S(2)}) copy-start(bf16[3,64,2,64,128]{4,3,2,1,0:T(8,128)(2,1)} %param.12) | copy-start | bytes 18874372
  68.6 19.5 %copy-start.5 = (bf16[64,64,512]{2,1,0:T(8,128)(2,1)S(1)}, bf16[64,64,512]{2,1,0:T(8,128)(2,1)}, u32[]{:S(2)}) copy-start(bf16[64,64,512]{2,1,0:T(8,128)(2,1)} %basis_hbm.1) | copy-start | bytes 12582916
  68.6 19.5 %copy-start.8 = (s32[1,16384]{1,0:T(1,128)S(1)}, s32[1,16384]{1,0:T(1,128)}, u32[]{:S(2)}) copy-start(s32[1,16384]{1,0:T(1,128)} %param.15) | copy-start | bytes 196612
  88.1 3.4 %copy-start.3 = (bf16[4,64,2,64,128]{4,3,2,1,0:T(8,128)(2,1)S(1)}, bf16[4,64,2,64,128]{4,3,2,1,0:T(8,128)(2,1)}, u32[]{:S(2)}) copy-start(bf16[4,64,2,64,128]{4,3,2,1,0:T(8,128)(2,1)} %factor_hbm.1) | copy-start | bytes 25165828
where the time goes:
time: 113 us
  Pallas kernels  47.2 us (42%)
  waiting for transfers between devices  25.6 us (23%)
  blocking collectives  17.8 us (16%)
  local copies, waits for them, and re-layouts  17 us (15%)
  starting transfers between devices  5.17 us (5%)
    ppermute x3, waiting for transfers between devices, local(): lax.ppermute(coef, 'lvl', [(i, i ^ 1 << level) for i in range(size)])  25.6 us
    pallas_call x1, Pallas kernels, target_fields(): pl.pallas_call(target_kernel, out_shape=jax.ShapeDtypeStruct((rhs, 2, cou...  21.5 us
    pallas_call x1, Pallas kernels, leaf_coefs(): pl.pallas_call(functools.partial(leaf_kernel, first, width), out_shape=ja...  20.8 us
    all_to_all x1, blocking collectives, local(): lax.all_to_all(coef, 'clu', split_axis=0, concat_axis=0, tiled=True)  17.8 us
    unnamed x20, local copies, waits for them, and re-layouts  17 us
    ppermute x3, starting transfers between devices, local(): lax.ppermute(coef, 'lvl', [(i, i ^ 1 << level) for i in range(size)])  5.17 us
    pallas_call x3, Pallas kernels, mix_level(): pl.pallas_call(functools.partial(mix_kernel, level, first), out_shape=jax...  5 us
  transfers between devices with their start and end apart: 3, of which 3 were waited for; matrix products, arithmetic and copies ran while one was open for 0% of the time, Pallas kernels for 0%

commit v1 on v0

v1 whole, which is shorter than its diff:
```python
import functools

import jax
import jax.numpy as jnp
from jax import lax
from jax.experimental import pallas as pl
from jax.experimental.pallas import tpu as pltpu
from jax.sharding import PartitionSpec as P

F32 = jnp.float32
BF16 = jnp.bfloat16
LANES = 128
PER_GROUP = 4
MANY = 8
PARTS = 2
EXTRA = 1
LEAF_LIMIT = 20


def lane_halves(shape):
    return lax.broadcasted_iota(jnp.int32, shape, 1) < shape[1] // 2


def packed_sum(first, second):
    turned = pltpu.roll(second, second.shape[1] // 2, 1)
    return first + jnp.where(lane_halves(first.shape), -turned, turned)


def sibling_rows(one, other):
    left = lane_halves(one.shape)
    half = one.shape[1] // 2
    real = jnp.where(left, one, pltpu.roll(other, half, 1))
    imag = jnp.where(left, pltpu.roll(one, half, 1), other)
    return jnp.concatenate([real, imag], axis=0)


def pairwise(steps, even, odd):
    def step(s, _):
        pl.when(s % 2 == 0)(functools.partial(even, s))
        pl.when(s % 2 == 1)(functools.partial(odd, s))
        return 0

    lax.fori_loop(0, steps, step, 0)


def gather_rows(order, table, segment, held, base):
    for q in range(LANES):
        held[pl.ds(base + q, 1), :] = table[pl.ds(order.at[q][segment], 1), :]


def leaf_boxes(order, ranks_ref, table, basis, coef_refs, held0, held1, mixed, columns):
    groups, width, points, packed = basis.shape
    rhs = columns // 2
    segments = points // LANES
    share = width // len(coef_refs)

    def collect(group, held):
        for place in range(width):
            for k in range(segments):
                segment = segments * (group * width + place) + k
                gather_rows(order, table, segment, held.at[place], k * LANES)

    def project(group, held):
        for place in range(width):
            rows = held[place].astype(BF16)[:, :columns]
            mixed[place] = lax.dot_general(
                rows, basis[group, place], (((0,), (0,)), ((), ())), preferred_element_type=F32
            )
        for place in range(width):
            out = packed_sum(
                mixed[place, pl.ds(0, rhs, 2), :], mixed[place, pl.ds(1, rhs, 2), :]
            )
            lane = lax.broadcasted_iota(jnp.int32, out.shape, 1) & (packed // 2 - 1)
            rank = ranks_ref[group * width + place]
            coef_refs[place // share][group, place % share] = jnp.where(
                lane < rank, out, 0.0
            ).astype(BF16)

    def even(s):
        project(jnp.maximum(s - 1, 0), held1)
        collect(s, held0)

    def odd(s):
        project(s - 1, held0)
        collect(s, held1)

    pairwise(groups, even, odd)
    project(groups - 1, held1)


def leaf_kernel(
    order_hbm, ranks_hbm, source_hbm, basis_hbm, *refs,
):
    loads_hbm, refs = refs[:EXTRA], refs[EXTRA:]
    coef_refs, refs = refs[:PARTS], refs[PARTS:]
    loads_ref, refs = refs[:EXTRA], refs[EXTRA:]
    table, turned, source, basis, held0, held1, mixed, order_vmem, order, ranks, sems = refs
    rhs, _, count = source.shape
    columns = 2 * rhs
    pieces = 4
    cut = count // pieces
    loads = [pltpu.make_async_copy(order_hbm, order_vmem, sems.at[0])]
    for k in range(pieces):
        spot = pl.ds(k * cut, cut)
        loads.append(
            pltpu.make_async_copy(
                source_hbm.at[:, :, spot], source.at[:, :, spot], sems.at[1 + k]
            )
        )
    load_basis = pltpu.make_async_copy(basis_hbm, basis, sems.at[pieces + 1])
    extra = [
        pltpu.make_async_copy(loads_hbm[k].at[0], loads_ref[k], sems.at[pieces + 4 + k])
        for k in range(EXTRA)
    ]
    load_ranks = pltpu.make_async_copy(ranks_hbm, ranks, sems.at[pieces + 2])
    load_order = pltpu.make_async_copy(turned, order, sems.at[pieces + 3])
    for load in loads:
        load.start()
    load_ranks.start()
    load_basis.start()
    for load in extra:
        load.start()
    loads[0].wait()
    turned[...] = order_vmem[...].T
    load_order.start()

    def fill(k, _):
        block = pl.ds(pl.multiple_of(k * LANES, LANES), LANES)
        table[block, :columns] = source[:, :, block].reshape(columns, LANES).T.astype(F32)
        return 0

    blocks = cut // LANES
    for k in range(pieces):
        loads[1 + k].wait()
        lax.fori_loop(k * blocks, (k + 1) * blocks, fill, 0, unroll=8)
    load_order.wait()
    load_ranks.wait()
    load_basis.wait()
    leaf_boxes(order, ranks, table, basis, coef_refs, held0, held1, mixed, columns)
    for load in extra:
        load.wait()


VMEM = pl.BlockSpec(memory_space=pltpu.VMEM)
ANYWHERE = pl.BlockSpec(memory_space=pl.ANY)


def in_hbm(x):
    return pltpu.with_memory_space_constraint(x, pltpu.HBM)


def in_vmem(x):
    return pltpu.with_memory_space_constraint(x, pltpu.VMEM)


def leaf_coefs(order, ranks, source, basis, extra):
    rhs, _, count = source.shape
    groups, width, points, packed = basis.shape
    segments = count // LANES
    coef = jax.ShapeDtypeStruct((groups, width // PARTS, rhs, packed), BF16)
    return pl.pallas_call(
        leaf_kernel,
        out_shape=[coef] * PARTS + [pltpu.VMEM(x.shape[1:], BF16) for x in extra],
        in_specs=[ANYWHERE] * (4 + EXTRA),
        out_specs=[VMEM] * (PARTS + EXTRA),
        scratch_shapes=[
            pltpu.VMEM((count, LANES), F32),
            pltpu.VMEM((LANES, segments), jnp.int32),
            pltpu.VMEM(source.shape, BF16),
            pltpu.VMEM(basis.shape, BF16),
            pltpu.VMEM((width, points, LANES), F32),
            pltpu.VMEM((width, points, LANES), F32),
            pltpu.VMEM((width, 2 * rhs, packed), F32),
            pltpu.VMEM((segments, LANES), jnp.int32),
            pltpu.SMEM((LANES, segments), jnp.int32),
            pltpu.SMEM(ranks.shape, jnp.int32),
            pltpu.SemaphoreType.DMA((8 + EXTRA,)),
        ],
        compiler_params=pltpu.CompilerParams(vmem_limit_bytes=LEAF_LIMIT << 20),
        name="leaf_coefs",
    )(*[in_hbm(x) for x in (order, ranks, source, basis) + tuple(extra)])


def mix_kernel(level, first, resident, upper_ref, own_ref, other_ref, factor_ref, *refs):
    groups, width = own_ref.shape[:2]
    upper = upper_ref[0]
    pieces = 1 if resident else 2
    cut = groups // pieces
    loads = []
    if not resident:
        *refs, factor, sems = refs
        for k in range(pieces):
            spot = pl.ds(k * cut, cut)
            loads.append(
                pltpu.make_async_copy(
                    factor_ref.at[level, spot, pl.ds(first, width)], factor.at[spot], sems.at[k]
                )
            )
        for load in loads:
            load.start()
    out_ref = refs[-1]
    offset = out_ref.shape[1] - width
    if offset:
        out_ref[:, :offset] = refs[0][...]

    def step(t, _):
        group, place = t // width, t % width
        rows = sibling_rows(own_ref[group, place], other_ref[group, place])
        mine = factor_ref.at[group, first + place] if resident else factor.at[group, place]
        weights = jnp.concatenate([mine[upper], mine[1 - upper]], axis=0)
        both = jnp.dot(rows, weights, preferred_element_type=F32)
        half = both.shape[0] // 2
        out_ref[group, offset + place] = packed_sum(both[:half], both[half:]).astype(BF16)
        return 0

    for k in range(pieces):
        if loads:
            loads[k].wait()
        lax.fori_loop(k * cut * width, (k + 1) * cut * width, step, 0, unroll=16)


def mix_level(upper, own, other, factors, level, first, before=(), resident=False):
    groups, width = own.shape[:2]
    full = width + sum(x.shape[1] for x in before)
    scratch = [
        pltpu.VMEM((groups, width) + factors.shape[3:], BF16),
        pltpu.SemaphoreType.DMA((2,)),
    ]
    return pl.pallas_call(
        functools.partial(mix_kernel, level, first, resident),
        out_shape=jax.ShapeDtypeStruct((groups, full) + own.shape[2:], BF16),
        in_specs=[pl.BlockSpec(memory_space=pltpu.SMEM), VMEM, VMEM]
        + [VMEM if resident else ANYWHERE] + [VMEM] * len(before),
        out_specs=VMEM,
        scratch_shapes=[] if resident else scratch,
        compiler_params=pltpu.CompilerParams(vmem_limit_bytes=6 << 20),
        name="mix_level",
    )(upper, own, other, in_vmem(factors) if resident else in_hbm(factors), *before)


def target_kernel(
    order_hbm, coef_ref, factor_hbm, basis_hbm, out_ref,
    factor, basis, table, work0, work1, rows, held0, held1, order_vmem, turned, order, sems,
):
    levels, boxes = factor.shape[:2]
    rhs, packed = coef_ref.shape[1:]
    rank = packed // 2
    points = basis.shape[2] // 2
    columns = 2 * rhs
    blocks = order_vmem.shape[0]
    load = pltpu.make_async_copy(order_hbm, order_vmem, sems.at[0])
    load.start()
    load_order = pltpu.make_async_copy(turned, order, sems.at[1])
    loads = [
        pltpu.make_async_copy(factor_hbm.at[k], factor.at[k], sems.at[2 + k])
        for k in range(levels)
    ]
    loads.append(pltpu.make_async_copy(basis_hbm, basis, sems.at[2 + levels]))
    for item in loads:
        item.start()
    load.wait()
    turned[...] = order_vmem[...].T
    load_order.start()
    low = 4
    source = coef_ref
    for k in range(levels):
        loads[k].wait()
        sink = (work0, work1)[k % 2]
        stride = low << k

        def pair(p, _, k=k, stride=stride, source=source, sink=sink):
            first = (p // stride) * (2 * stride) + p % stride
            second = first + stride
            lhs = sibling_rows(source[first], source[second])
            for box in (first, second):
                weights = factor[k, box].reshape(packed, packed)
                both = jnp.dot(lhs, weights, preferred_element_type=F32)
                sink[box] = packed_sum(both[:rhs], both[rhs:]).astype(BF16)
            return 0

        lax.fori_loop(0, boxes // 2, pair, 0, unroll=32)
        source = sink

    loads[levels].wait()

    def expand(box, _):
        coef = source[box].astype(F32)
        buf = rows.at[box % 16]
        buf[pl.ds(0, rhs, 2), :] = jnp.where(lane_halves(coef.shape), coef, -coef)
        buf[pl.ds(1, rhs, 2), :] = pltpu.roll(coef, rank, 1)
        weights = basis[box]
        weights = jnp.concatenate([weights[:, :points], weights[:, points:]], axis=0)
        field = jnp.dot(buf[...].astype(BF16), weights, preferred_element_type=F32).astype(BF16)
        spot = pl.ds(pl.multiple_of(box * points, points), points)
        table[spot, :columns] = field.T.astype(F32)
        return 0

    lax.fori_loop(0, boxes, expand, 0, unroll=16)
    load_order.wait()
    many = held0.shape[0]

    def collect(s, held):
        for part in range(many):
            gather_rows(order, table, many * s + part, held.at[part], 0)

    def place(s, held):
        for part in range(many):
            values = held[part].astype(BF16)[:, :columns].T
            spot = pl.ds(pl.multiple_of((many * s + part) * LANES, LANES), LANES)
            out_ref[:, :, spot] = values.reshape(rhs, 2, LANES)

    def even(s):
        place(jnp.maximum(s - 1, 0), held1)
        collect(s, held0)

    def odd(s):
        place(s - 1, held0)
        collect(s, held1)

    pairwise(blocks // many, even, odd)
    place(blocks // many - 1, held1)


def target_fields(order, coef, factors, basis):
    boxes, rhs, packed = coef.shape
    points = basis.shape[2] // 2
    count = boxes * points
    return pl.pallas_call(
        target_kernel,
        out_shape=jax.ShapeDtypeStruct((rhs, 2, count), BF16),
        in_specs=[ANYWHERE, VMEM, ANYWHERE, ANYWHERE],
        out_specs=VMEM,
        scratch_shapes=[
            pltpu.VMEM(factors.shape, BF16),
            pltpu.VMEM(basis.shape, BF16),
            pltpu.VMEM((count, LANES), F32),
            pltpu.VMEM(coef.shape, BF16),
            pltpu.VMEM(coef.shape, BF16),
            pltpu.VMEM((16, 2 * rhs, packed), F32),
            pltpu.VMEM((MANY, LANES, LANES), F32),
            pltpu.VMEM((MANY, LANES, LANES), F32),
            pltpu.VMEM((count // LANES, LANES), jnp.int32),
            pltpu.VMEM((LANES, count // LANES), jnp.int32),
            pltpu.SMEM((LANES, count // LANES), jnp.int32),
            pltpu.SemaphoreType.DMA((3 + factors.shape[0],)),
        ],
        compiler_params=pltpu.CompilerParams(vmem_limit_bytes=32 << 20),
        name="target_fields",
    )(in_hbm(order), coef, in_hbm(factors), in_hbm(basis))


def local(
    sources,
    source_order,
    leaf_basis,
    leaf_ranks,
    source_factors,
    target_factors,
    target_basis,
    target_order,
):
    boxes, points, packed = leaf_basis.shape
    rhs, _, count = sources.shape
    groups = lax.axis_size("clu")
    per_group = boxes // groups
    order_in = source_order.reshape(count // LANES, LANES)
    order_out = target_order.reshape(count // LANES, LANES)
    basis = leaf_basis.reshape((groups, per_group) + leaf_basis.shape[1:])
    levels = source_factors.shape[0]
    factors = source_factors.reshape((levels, groups, per_group) + source_factors.shape[2:])
    size = lax.axis_size("lvl")
    uppers = [
        (lax.axis_index("lvl") >> level & 1).reshape(1).astype(jnp.int32)
        for level in range(levels)
    ]
    outs = leaf_coefs(order_in, leaf_ranks, sources, basis, (factors,))
    coefs = list(outs[:PARTS])
    head = outs[PARTS]
    width = per_group // PARTS
    for level in range(levels):
        swap = [(i, i ^ 1 << level) for i in range(size)]
        for k in range(PARTS):
            other = lax.ppermute(coefs[k], "lvl", swap)
            last = level == levels - 1 and k == PARTS - 1
            coefs[k] = mix_level(
                uppers[level], coefs[k], other, factors if level else head, level, k * width,
                coefs[:k] if last else (), level == 0,
            )
    coef = lax.all_to_all(coefs[-1], "clu", split_axis=0, concat_axis=0, tiled=True)
    coef = coef.reshape(boxes, rhs, packed)
    return target_fields(order_out, coef, target_factors, target_basis)


def solution(mesh):
    both = ("lvl", "clu")
    placed = (
        P(None, None, both),
        P(both, None),
        P(both, None, None),
        P(both),
        P(None, both, None, None, None),
        P(None, both, None, None, None),
        P(both, None, None),
        P(both, None),
    )
    return jax.shard_map(
        local, mesh=mesh, in_specs=placed, out_specs=P(None, None, both), check_vma=False
    )
```

time: 113 us -> 89.1 us (0.79)
  local copies, waits for them, and re-layouts: 17 us -> 0 us
  waiting for transfers between devices: 25.6 us -> 13.1 us
  starting transfers between devices: 5.17 us -> 9.87 us
    unnamed x20 -> x0, local copies, waits for them, and re-layouts: 17 us -> none
    ppermute x3 -> x6, waiting for transfers between devices: 25.6 us -> 13.1 us  [local(): other = lax.ppermute(coefs[k], 'lvl', swap)]
    ppermute x3 -> x6, starting transfers between devices: 5.17 us -> 9.87 us  [local(): other = lax.ppermute(coefs[k], 'lvl', swap)]
    pallas_call x1, Pallas kernels: 21.5 us -> 20.1 us  [target_fields(): pl.pallas_call(target_kernel, out_shape=jax.ShapeDtypeStruct((rhs, 2, cou...]
    pallas_call x4 -> x7, Pallas kernels: 25.8 us -> 26.8 us  [the longest x1 17.8 us: leaf_coefs(): pl.pallas_call(leaf_kernel, out_shape=[coef] * PARTS + [pltpu.VMEM(x.shap...]
  transfers between devices with their start and end apart: 3 -> 6, of which waited for: 3 -> 4; matrix products, arithmetic and copies ran while one was open for 0% -> 0% of each run, Pallas kernels for 0% -> 8%
where the time goes in v1:
time: 89.1 us; the launch traced here: 88.8 us
  Pallas kernels  46.9 us (53%)
  blocking collectives  18.7 us (21%)
  waiting for transfers between devices  13.1 us (15%)
  starting transfers between devices  9.87 us (11%)
    pallas_call x1, Pallas kernels, target_fields(): pl.pallas_call(target_kernel, out_shape=jax.ShapeDtypeStruct((rhs, 2, cou...  20.1 us
    all_to_all x1, blocking collectives, local(): lax.all_to_all(coefs[-1], 'clu', split_axis=0, concat_axis=0, tiled=True)  18.7 us
    pallas_call x1, Pallas kernels, leaf_coefs(): pl.pallas_call(leaf_kernel, out_shape=[coef] * PARTS + [pltpu.VMEM(x.shap...  17.8 us
    ppermute x6, waiting for transfers between devices, local(): other = lax.ppermute(coefs[k], 'lvl', swap)  13.1 us
    ppermute x6, starting transfers between devices, local(): other = lax.ppermute(coefs[k], 'lvl', swap)  9.87 us
    pallas_call x6, Pallas kernels, mix_level(): pl.pallas_call(functools.partial(mix_kernel, level, first, resident), out...  9.08 us
  transfers between devices with their start and end apart: 6, of which 4 were waited for; matrix products, arithmetic and copies ran while one was open for 0% of the time, Pallas kernels for 8%

profile of v1, /device:TPU:0, one launch (start us, length us, event | category | flops | bytes accessed | tf_op | source)
XLA Modules:
  0.0 88.8 jit_solution(14385453243244010933)
XLA Ops:
  0.0 17.8 %leaf_coefs.1 = (bf16[16,2,32,128]{3,2,1,0:T(8,128)(2,1)S(1)}, bf16[16,2,32,128]{3,2,1,0:T(8,128)(2,1)S(1)}, bf16[16,4,2,64,128]{4,3,2,1,0:T(8,128)(2,1)S(1)}) custom-call(s32[128,128]{1,0:T(8,128)} %bitcast.15, s32[64]{0:T(128)} %ranks_hbm.1, bf16[32,2,16384]{2,1,0:T(2,128)(2,1)} %source_hbm.1, bf16[16,4,256,128]{3,2,1,0:T(8,128)(2,1)} %bitcast.14, ...), custom_call_target="tpu_custom_call" | custom-call | tf_op jit(solution)/shard_map/leaf_coefs/pallas_call | solution.py:161
  17.8 0.1 collective-permute-start.3
  17.9 0.5 collective-permute-start
  18.4 1.0 %collective-permute-done.3.other_ref = bf16[16,2,32,128]{3,2,1,0:T(8,128)(2,1)S(1)} collective-permute-done((bf16[16,2,32,128]{3,2,1,0:T(8,128)(2,1)S(1)}, bf16[16,2,32,128]{3,2,1,0:T(8,128)(2,1)S(1)}, u32[]{:S(2)}, u32[]{:S(2)}) %collective-permute-start.3) | collective-permute-done | bytes 262176 | tf_op jit(solution)/shard_map/ppermute | solution.py:383
  19.4 0.8 mix_level.8.own_ref
  20.2 1.7 %collective-permute-start.4 = (bf16[16,2,32,128]{3,2,1,0:T(8,128)(2,1)S(1)}, bf16[16,2,32,128]{3,2,1,0:T(8,128)(2,1)S(1)}, u32[]{:S(2)}, u32[]{:S(2)}) collective-permute-start(bf16[16,2,32,128]{3,2,1,0:T(8,128)(2,1)S(1)} %mix_level.8.own_ref), channel_id=1, source_target_pairs={{0,32},{16,48},{32,0},{48,16},{64,96},{80,112},{96,64},{112,80},{1... | collective-permute-start | bytes 786440 | tf_op jit(solution)/shard_map/ppermute | solution.py:383
  22.0 0.0 collective-permute-done.other_ref
  22.0 0.8 mix_level.6.own_ref
  22.8 0.4 collective-permute-start.1
  23.2 6.2 %collective-permute-done.4.other_ref = bf16[16,2,32,128]{3,2,1,0:T(8,128)(2,1)S(1)} collective-permute-done((bf16[16,2,32,128]{3,2,1,0:T(8,128)(2,1)S(1)}, bf16[16,2,32,128]{3,2,1,0:T(8,128)(2,1)S(1)}, u32[]{:S(2)}, u32[]{:S(2)}) %collective-permute-start.4) | collective-permute-done | bytes 262176 | tf_op jit(solution)/shard_map/ppermute | solution.py:383
  29.4 1.9 %mix_level.9.own_ref = bf16[16,2,32,128]{3,2,1,0:T(8,128)(2,1)S(1)} custom-call(s32[1]{0:T(128)} %bitcast.2.upper_ref, bf16[16,2,32,128]{3,2,1,0:T(8,128)(2,1)S(1)} %mix_level.8.own_ref, bf16[16,2,32,128]{3,2,1,0:T(8,128)(2,1)S(1)} %collective-permute-done.4.other_ref, bf16[3,16,4,2,64,128]{5,4,3,2,1,0:T(8,128)(2,1)} %bitcast.10), custom_call_target="tpu_custom_call" | custom-call | tf_op jit(solution)/shard_map/mix_level/pallas_call | solution.py:229
  31.3 3.4 %collective-permute-start.5 = (bf16[16,2,32,128]{3,2,1,0:T(8,128)(2,1)S(1)}, bf16[16,2,32,128]{3,2,1,0:T(8,128)(2,1)S(1)}, u32[]{:S(2)}, u32[]{:S(2)}) collective-permute-start(bf16[16,2,32,128]{3,2,1,0:T(8,128)(2,1)S(1)} %mix_level.9.own_ref), channel_id=1, source_target_pairs={{0,64},{16,80},{32,96},{48,112},{64,0},{80,16},{96,32},{112,48},{1... | collective-permute-start | bytes 786440 | tf_op jit(solution)/shard_map/ppermute | solution.py:383
  34.7 0.0 collective-permute-done.1.other_ref
  34.7 1.9 %mix_level.7.own_ref = bf16[16,2,32,128]{3,2,1,0:T(8,128)(2,1)S(1)} custom-call(s32[1]{0:T(128)} %bitcast.2.upper_ref, bf16[16,2,32,128]{3,2,1,0:T(8,128)(2,1)S(1)} %mix_level.6.own_ref, bf16[16,2,32,128]{3,2,1,0:T(8,128)(2,1)S(1)} %collective-permute-done.1.other_ref, bf16[3,16,4,2,64,128]{5,4,3,2,1,0:T(8,128)(2,1)} %bitcast.11), custom_call_target="tpu_custom_call" | custom-call | tf_op jit(solution)/shard_map/mix_level/pallas_call | solution.py:229
  36.5 3.7 %collective-permute-start.2 = (bf16[16,2,32,128]{3,2,1,0:T(8,128)(2,1)S(1)}, bf16[16,2,32,128]{3,2,1,0:T(8,128)(2,1)S(1)}, u32[]{:S(2)}, u32[]{:S(2)}) collective-permute-start(bf16[16,2,32,128]{3,2,1,0:T(8,128)(2,1)S(1)} %mix_level.7.own_ref), channel_id=1, source_target_pairs={{0,64},{16,80},{32,96},{48,112},{64,0},{80,16},{96,32},{112,48},{1... | collective-permute-start | bytes 786440 | tf_op jit(solution)/shard_map/ppermute | solution.py:383
  40.3 2.9 %collective-permute-done.5.other_ref = bf16[16,2,32,128]{3,2,1,0:T(8,128)(2,1)S(1)} collective-permute-done((bf16[16,2,32,128]{3,2,1,0:T(8,128)(2,1)S(1)}, bf16[16,2,32,128]{3,2,1,0:T(8,128)(2,1)S(1)}, u32[]{:S(2)}, u32[]{:S(2)}) %collective-permute-start.5) | collective-permute-done | bytes 262176 | tf_op jit(solution)/shard_map/ppermute | solution.py:383
  43.2 1.9 %mix_level.10.refs_0_ = bf16[16,2,32,128]{3,2,1,0:T(8,128)(2,1)S(1)} custom-call(s32[1]{0:T(128)} %bitcast.1.upper_ref, bf16[16,2,32,128]{3,2,1,0:T(8,128)(2,1)S(1)} %mix_level.9.own_ref, bf16[16,2,32,128]{3,2,1,0:T(8,128)(2,1)S(1)} %collective-permute-done.5.other_ref, bf16[3,16,4,2,64,128]{5,4,3,2,1,0:T(8,128)(2,1)} %bitcast.12), custom_call_target="tpu_custom_call" | custom-call | tf_op jit(solution)/shard_map/mix_level/pallas_call | solution.py:229
  45.1 2.9 %collective-permute-done.2.other_ref = bf16[16,2,32,128]{3,2,1,0:T(8,128)(2,1)S(1)} collective-permute-done((bf16[16,2,32,128]{3,2,1,0:T(8,128)(2,1)S(1)}, bf16[16,2,32,128]{3,2,1,0:T(8,128)(2,1)S(1)}, u32[]{:S(2)}, u32[]{:S(2)}) %collective-permute-start.2) | collective-permute-done | bytes 262176 | tf_op jit(solution)/shard_map/ppermute | solution.py:383
  48.0 1.9 %mix_level.11 = bf16[16,4,32,128]{3,2,1,0:T(8,128)(2,1)S(1)} custom-call(s32[1]{0:T(128)} %bitcast.1.upper_ref, bf16[16,2,32,128]{3,2,1,0:T(8,128)(2,1)S(1)} %mix_level.7.own_ref, bf16[16,2,32,128]{3,2,1,0:T(8,128)(2,1)S(1)} %collective-permute-done.2.other_ref, bf16[3,16,4,2,64,128]{5,4,3,2,1,0:T(8,128)(2,1)} %bitcast.13, ...), custom_call_target="tpu_custom_call" | custom-call | tf_op jit(solution)/shard_map/mix_level/pallas_call | solution.py:229
  49.9 18.7 %all_to_all.5 = bf16[16,4,32,128]{3,2,1,0:T(8,128)(2,1)S(1)} all-to-all(bf16[16,4,32,128]{3,2,1,0:T(8,128)(2,1)S(1)} %mix_level.11), channel_id=1, replica_groups=mesh['lvl'=8,'clu'=16] {'clu'}, dimensions={0} | all-to-all | bytes 1048576 | tf_op jit(solution)/shard_map/all_to_all | solution.py:389
  68.6 20.1 %target_fields.1 = bf16[32,2,16384]{2,1,0:T(2,128)(2,1)} custom-call(s32[128,128]{1,0:T(8,128)} %bitcast.16, bf16[64,32,128]{2,1,0:T(8,128)(2,1)S(1)} %bitcast.8, bf16[4,64,2,64,128]{4,3,2,1,0:T(8,128)(2,1)} %factor_hbm.1, bf16[64,64,512]{2,1,0:T(8,128)(2,1)} %basis_hbm.1), custom_call_target="tpu_custom_call" | custom-call | tf_op jit(solution)/shard_map/target_fields/pallas_call | solution.py:328
Async XLA Ops:
  17.8 1.6 %collective-permute-start.3 = (bf16[16,2,32,128]{3,2,1,0:T(8,128)(2,1)S(1)}, bf16[16,2,32,128]{3,2,1,0:T(8,128)(2,1)S(1)}, u32[]{:S(2)}, u32[]{:S(2)}) collective-permute-start(bf16[16,2,32,128]{3,2,1,0:T(8,128)(2,1)S(1)} %get-tuple-element.10.own_ref), channel_id=1, source_target_pairs={{0,16},{16,0},{32,48},{48,32},{64,80},{80,64},{96,112},{112,96},{1... | collective-permute-start | bytes 786440 | tf_op jit(solution)/shard_map/ppermute | solution.py:383
  17.9 4.1 %collective-permute-start = (bf16[16,2,32,128]{3,2,1,0:T(8,128)(2,1)S(1)}, bf16[16,2,32,128]{3,2,1,0:T(8,128)(2,1)S(1)}, u32[]{:S(2)}, u32[]{:S(2)}) collective-permute-start(bf16[16,2,32,128]{3,2,1,0:T(8,128)(2,1)S(1)} %get-tuple-element.8.own_ref), channel_id=1, source_target_pairs={{0,16},{16,0},{32,48},{48,32},{64,80},{80,64},{96,112},{112,96},{1... | collective-permute-start | bytes 786440 | tf_op jit(solution)/shard_map/ppermute | solution.py:383
  20.2 9.2 %collective-permute-start.4 = (bf16[16,2,32,128]{3,2,1,0:T(8,128)(2,1)S(1)}, bf16[16,2,32,128]{3,2,1,0:T(8,128)(2,1)S(1)}, u32[]{:S(2)}, u32[]{:S(2)}) collective-permute-start(bf16[16,2,32,128]{3,2,1,0:T(8,128)(2,1)S(1)} %mix_level.8.own_ref), channel_id=1, source_target_pairs={{0,32},{16,48},{32,0},{48,16},{64,96},{80,112},{96,64},{112,80},{1... | collective-permute-start | bytes 786440 | tf_op jit(solution)/shard_map/ppermute | solution.py:383
  22.8 11.9 %collective-permute-start.1 = (bf16[16,2,32,128]{3,2,1,0:T(8,128)(2,1)S(1)}, bf16[16,2,32,128]{3,2,1,0:T(8,128)(2,1)S(1)}, u32[]{:S(2)}, u32[]{:S(2)}) collective-permute-start(bf16[16,2,32,128]{3,2,1,0:T(8,128)(2,1)S(1)} %mix_level.6.own_ref), channel_id=1, source_target_pairs={{0,32},{16,48},{32,0},{48,16},{64,96},{80,112},{96,64},{112,80},{1... | collective-permute-start | bytes 786440 | tf_op jit(solution)/shard_map/ppermute | solution.py:383
  31.3 11.9 %collective-permute-start.5 = (bf16[16,2,32,128]{3,2,1,0:T(8,128)(2,1)S(1)}, bf16[16,2,32,128]{3,2,1,0:T(8,128)(2,1)S(1)}, u32[]{:S(2)}, u32[]{:S(2)}) collective-permute-start(bf16[16,2,32,128]{3,2,1,0:T(8,128)(2,1)S(1)} %mix_level.9.own_ref), channel_id=1, source_target_pairs={{0,64},{16,80},{32,96},{48,112},{64,0},{80,16},{96,32},{112,48},{1... | collective-permute-start | bytes 786440 | tf_op jit(solution)/shard_map/ppermute | solution.py:383
  36.5 11.5 %collective-permute-start.2 = (bf16[16,2,32,128]{3,2,1,0:T(8,128)(2,1)S(1)}, bf16[16,2,32,128]{3,2,1,0:T(8,128)(2,1)S(1)}, u32[]{:S(2)}, u32[]{:S(2)}) collective-permute-start(bf16[16,2,32,128]{3,2,1,0:T(8,128)(2,1)S(1)} %mix_level.7.own_ref), channel_id=1, source_target_pairs={{0,64},{16,80},{32,96},{48,112},{64,0},{80,16},{96,32},{112,48},{1... | collective-permute-start | bytes 786440 | tf_op jit(solution)/shard_map/ppermute | solution.py:383

commit v2 on v1

v2 whole, which is shorter than its diff:
```python
import functools

import jax
import jax.numpy as jnp
from jax import lax
from jax.experimental import pallas as pl
from jax.experimental.pallas import tpu as pltpu
from jax.sharding import PartitionSpec as P

F32 = jnp.float32
BF16 = jnp.bfloat16
LANES = 128
PER_GROUP = 4
MANY = 8
PARTS = 2
EXTRA = 1
LEAF_LIMIT = 32
BATCH = 8


def lane_halves(shape):
    return lax.broadcasted_iota(jnp.int32, shape, 1) < shape[1] // 2


def packed_sum(first, second):
    turned = pltpu.roll(second, second.shape[1] // 2, 1)
    return first + jnp.where(lane_halves(first.shape), -turned, turned)


def sibling_rows(one, other):
    left = lane_halves(one.shape)
    half = one.shape[1] // 2
    real = jnp.where(left, one, pltpu.roll(other, half, 1))
    imag = jnp.where(left, pltpu.roll(one, half, 1), other)
    return jnp.concatenate([real, imag], axis=0)


def pairwise(steps, even, odd):
    def step(s, _):
        pl.when(s % 2 == 0)(functools.partial(even, s))
        pl.when(s % 2 == 1)(functools.partial(odd, s))
        return 0

    lax.fori_loop(0, steps, step, 0)


def gather_rows(order, table, segment, held, base):
    for q in range(LANES):
        held[pl.ds(base + q, 1), :] = table[pl.ds(order.at[q][segment], 1), :]


def leaf_boxes(order, ranks_ref, table, basis, coef_refs, held, mixed, columns):
    groups, width, points, packed = basis.shape
    rhs = columns // 2
    segments = points // LANES
    share = width // len(coef_refs)

    def collect(group, _):
        for place in range(width):
            for k in range(segments):
                segment = segments * (group * width + place) + k
                gather_rows(order, table, segment, held.at[group, place], k * LANES)
        return 0

    lax.fori_loop(0, groups, collect, 0)
    lane = lax.broadcasted_iota(jnp.int32, (rhs, packed), 1) & (packed // 2 - 1)

    def project(step, _):
        boxes = [(step * BATCH + g, g, place) for g in range(BATCH) for place in range(width)]
        for group, g, place in boxes:
            rows = held[group, place].astype(BF16)[:, :columns]
            mixed[g, place] = lax.dot_general(
                rows, basis[group, place], (((0,), (0,)), ((), ())), preferred_element_type=F32
            )
        for group, g, place in boxes:
            out = packed_sum(
                mixed[g, place, pl.ds(0, rhs, 2), :], mixed[g, place, pl.ds(1, rhs, 2), :]
            )
            rank = ranks_ref[group * width + place]
            coef_refs[place // share][group, place % share] = jnp.where(
                lane < rank, out, 0.0
            ).astype(BF16)
        return 0

    lax.fori_loop(0, groups // BATCH, project, 0)


def leaf_kernel(
    order_hbm, ranks_hbm, source_hbm, basis_hbm, *refs,
):
    loads_hbm, refs = refs[:EXTRA], refs[EXTRA:]
    coef_refs, refs = refs[:PARTS], refs[PARTS:]
    loads_ref, refs = refs[:EXTRA], refs[EXTRA:]
    table, turned, source, basis, held, mixed, order_vmem, order, ranks, sems = refs
    rhs, _, count = source.shape
    columns = 2 * rhs
    pieces = 4
    cut = count // pieces
    loads = [pltpu.make_async_copy(order_hbm, order_vmem, sems.at[0])]
    for k in range(pieces):
        spot = pl.ds(k * cut, cut)
        loads.append(
            pltpu.make_async_copy(
                source_hbm.at[:, :, spot], source.at[:, :, spot], sems.at[1 + k]
            )
        )
    load_basis = pltpu.make_async_copy(basis_hbm, basis, sems.at[pieces + 1])
    extra = [
        pltpu.make_async_copy(loads_hbm[k].at[0], loads_ref[k], sems.at[pieces + 4 + k])
        for k in range(EXTRA)
    ]
    load_ranks = pltpu.make_async_copy(ranks_hbm, ranks, sems.at[pieces + 2])
    load_order = pltpu.make_async_copy(turned, order, sems.at[pieces + 3])
    for load in loads:
        load.start()
    load_ranks.start()
    load_basis.start()
    for load in extra:
        load.start()
    loads[0].wait()
    turned[...] = order_vmem[...].T
    load_order.start()

    def fill(k, _):
        block = pl.ds(pl.multiple_of(k * LANES, LANES), LANES)
        table[block, :columns] = source[:, :, block].reshape(columns, LANES).T.astype(F32)
        return 0

    blocks = cut // LANES
    for k in range(pieces):
        loads[1 + k].wait()
        lax.fori_loop(k * blocks, (k + 1) * blocks, fill, 0, unroll=8)
    load_order.wait()
    load_ranks.wait()
    load_basis.wait()
    leaf_boxes(order, ranks, table, basis, coef_refs, held, mixed, columns)
    for load in extra:
        load.wait()


VMEM = pl.BlockSpec(memory_space=pltpu.VMEM)
ANYWHERE = pl.BlockSpec(memory_space=pl.ANY)


def in_hbm(x):
    return pltpu.with_memory_space_constraint(x, pltpu.HBM)


def in_vmem(x):
    return pltpu.with_memory_space_constraint(x, pltpu.VMEM)


def leaf_coefs(order, ranks, source, basis, extra):
    rhs, _, count = source.shape
    groups, width, points, packed = basis.shape
    segments = count // LANES
    coef = jax.ShapeDtypeStruct((groups, width // PARTS, rhs, packed), BF16)
    return pl.pallas_call(
        leaf_kernel,
        out_shape=[coef] * PARTS + [pltpu.VMEM(x.shape[1:], BF16) for x in extra],
        in_specs=[ANYWHERE] * (4 + EXTRA),
        out_specs=[VMEM] * (PARTS + EXTRA),
        scratch_shapes=[
            pltpu.VMEM((count, LANES), F32),
            pltpu.VMEM((LANES, segments), jnp.int32),
            pltpu.VMEM(source.shape, BF16),
            pltpu.VMEM(basis.shape, BF16),
            pltpu.VMEM((groups, width, points, LANES), F32),
            pltpu.VMEM((BATCH, width, 2 * rhs, packed), F32),
            pltpu.VMEM((segments, LANES), jnp.int32),
            pltpu.SMEM((LANES, segments), jnp.int32),
            pltpu.SMEM(ranks.shape, jnp.int32),
            pltpu.SemaphoreType.DMA((8 + EXTRA,)),
        ],
        compiler_params=pltpu.CompilerParams(vmem_limit_bytes=LEAF_LIMIT << 20),
        name="leaf_coefs",
    )(*[in_hbm(x) for x in (order, ranks, source, basis) + tuple(extra)])


def mix_kernel(level, first, resident, joined, ahead, upper_ref, own_ref, other_ref, factor_ref, *refs):
    groups, width = own_ref.shape[:2]
    upper = upper_ref[0]
    before, refs = refs[:joined], refs[joined:]
    sources, refs = refs[: len(ahead)], refs[len(ahead) :]
    out_ref, refs = refs[0], refs[1:]
    sinks, refs = refs[: len(ahead)], refs[len(ahead) :]
    *factor, sems = refs
    pieces = 1 if resident else 2
    cut = groups // pieces
    loads = []
    if not resident:
        for k in range(pieces):
            spot = pl.ds(k * cut, cut)
            loads.append(
                pltpu.make_async_copy(
                    factor_ref.at[level, spot, pl.ds(first, width)], factor[0].at[spot], sems.at[k]
                )
            )
    later = [
        pltpu.make_async_copy(
            sources[k].at[row, :, pl.ds(at, size)], sinks[k], sems.at[pieces + k]
        )
        for k, (row, at, size) in enumerate(ahead)
    ]
    for load in loads + later:
        load.start()
    offset = out_ref.shape[1] - width
    if joined:
        out_ref[:, :offset] = before[0][...]

    def step(t, _):
        group, place = t // width, t % width
        rows = sibling_rows(own_ref[group, place], other_ref[group, place])
        mine = factor_ref.at[group, first + place] if resident else factor[0].at[group, place]
        weights = jnp.concatenate([mine[upper], mine[1 - upper]], axis=0)
        both = jnp.dot(rows, weights, preferred_element_type=F32)
        half = both.shape[0] // 2
        out_ref[group, offset + place] = packed_sum(both[:half], both[half:]).astype(BF16)
        return 0

    for k in range(pieces):
        if loads:
            loads[k].wait()
        lax.fori_loop(k * cut * width, (k + 1) * cut * width, step, 0, unroll=cut * width)
    for load in later:
        load.wait()


def mix_level(upper, own, other, factors, level, first, resident=False, before=(), ahead=()):
    groups, width = own.shape[:2]
    full = width + sum(x.shape[1] for x in before)
    scratch = [] if resident else [pltpu.VMEM((groups, width) + factors.shape[3:], BF16)]
    out = jax.ShapeDtypeStruct((groups, full) + own.shape[2:], BF16)
    outs = pl.pallas_call(
        functools.partial(mix_kernel, level, first, resident, len(before), [x[1:] for x in ahead]),
        out_shape=[out] + [pltpu.VMEM((groups, x[3]) + x[0].shape[3:], BF16) for x in ahead],
        in_specs=[pl.BlockSpec(memory_space=pltpu.SMEM), VMEM, VMEM]
        + [VMEM if resident else ANYWHERE]
        + [VMEM] * len(before)
        + [ANYWHERE] * len(ahead),
        out_specs=[VMEM] * (1 + len(ahead)),
        scratch_shapes=scratch + [pltpu.SemaphoreType.DMA((2 + len(ahead),))],
        compiler_params=pltpu.CompilerParams(vmem_limit_bytes=6 << 20),
        name="mix_level",
    )(
        upper, own, other, in_vmem(factors) if resident else in_hbm(factors),
        *before, *[in_hbm(x[0]) for x in ahead],
    )
    return outs[0], list(outs[1:])


def target_levels(coef_ref, head, factor, basis, table, work, rows, loads):
    groups, width, rhs, packed = coef_ref.shape
    points = basis.shape[3] // 2
    columns = 2 * rhs
    source = coef_ref
    for k in range(factor.shape[0] + 1):
        if k:
            loads[k - 1].wait()
        weights_ref = factor.at[k - 1] if k else head
        sink = work.at[k % 2]
        stride = 1 << k

        def pair(p, _, weights_ref=weights_ref, stride=stride, source=source, sink=sink):
            t, place = p // width, p % width
            low = (t // stride) * (2 * stride) + t % stride
            high = low + stride
            lhs = sibling_rows(source[low, place], source[high, place])
            for group in (low, high):
                weights = weights_ref[group, place].reshape(packed, packed)
                both = jnp.dot(lhs, weights, preferred_element_type=F32)
                sink[group, place] = packed_sum(both[:rhs], both[rhs:]).astype(BF16)
            return 0

        lax.fori_loop(0, groups * width // 2, pair, 0, unroll=32)
        source = sink
    loads[-1].wait()

    def expand(t, _):
        group, place = t // width, t % width
        coef = source[group, place].astype(F32)
        buf = rows.at[t % rows.shape[0]]
        buf[pl.ds(0, rhs, 2), :] = jnp.where(lane_halves(coef.shape), coef, -coef)
        buf[pl.ds(1, rhs, 2), :] = pltpu.roll(coef, packed // 2, 1)
        weights = basis[group, place]
        weights = jnp.concatenate([weights[:, :points], weights[:, points:]], axis=0)
        field = jnp.dot(buf[...].astype(BF16), weights, preferred_element_type=F32).astype(BF16)
        table[group, place, :, :columns] = field.T.astype(F32)
        return 0

    lax.fori_loop(0, groups * width, expand, 0, unroll=16)


def target_kernel(
    order_hbm, coef_ref, head, factor_hbm, basis_hbm, out_hbm,
    factor, basis, work, rows, table, held0, held1, order_vmem, turned, order, out, sems, out_sems,
):
    levels = factor.shape[0]
    rhs = coef_ref.shape[2]
    columns = 2 * rhs
    blocks = order_vmem.shape[0]
    load = pltpu.make_async_copy(order_hbm, order_vmem, sems.at[levels + 1])
    load_order = pltpu.make_async_copy(turned, order, sems.at[levels + 2])
    loads = [
        pltpu.make_async_copy(factor_hbm.at[k + 1], factor.at[k], sems.at[k])
        for k in range(levels)
    ]
    loads.append(pltpu.make_async_copy(basis_hbm, basis, sems.at[levels]))
    load.start()
    for item in loads:
        item.start()
    load.wait()
    turned[...] = order_vmem[...].T
    load_order.start()
    target_levels(coef_ref, head, factor, basis, table, work, rows, loads)
    load_order.wait()
    flat = table.reshape(blocks * LANES, LANES)
    many = held0.shape[0]

    def place_part(s, part, held):
        values = held[part].astype(BF16)[:, :columns].T
        spot = pl.ds(pl.multiple_of((many * s + part) * LANES, LANES), LANES)
        out[:, :, spot] = values.reshape(rhs, 2, LANES)

    def both(s, old, new):
        for part in range(many):
            place_part(jnp.maximum(s - 1, 0), part, old)
        for part in range(many):
            gather_rows(order, flat, many * s + part, new.at[part], 0)

    def store(s):
        size = many * LANES
        spot = pl.ds(pl.multiple_of(s * size, size), size)
        return pltpu.make_async_copy(out.at[:, :, spot], out_hbm.at[:, :, spot], out_sems.at[s])

    def even(s):
        both(s, held1, held0)
        pl.when(s > 0)(lambda: store(s - 1).start())

    def odd(s):
        both(s, held0, held1)
        store(s - 1).start()

    steps = blocks // many
    pairwise(steps, even, odd)
    for part in range(many):
        place_part(steps - 1, part, held1)
    store(steps - 1).start()
    for s in range(steps):
        store(s).wait()


def target_fields(order, coef, head, factors, basis):
    groups, width, rhs, packed = coef.shape
    levels, points = factors.shape[0] - 1, basis.shape[3] // 2
    blocks = order.shape[0]
    return pl.pallas_call(
        target_kernel,
        out_shape=jax.ShapeDtypeStruct((rhs, 2, blocks * LANES), BF16),
        in_specs=[ANYWHERE, VMEM, VMEM, ANYWHERE, ANYWHERE],
        out_specs=ANYWHERE,
        scratch_shapes=[
            pltpu.VMEM((levels,) + factors.shape[1:], BF16),
            pltpu.VMEM(basis.shape, BF16),
            pltpu.VMEM((2,) + coef.shape, BF16),
            pltpu.VMEM((16, 2 * rhs, packed), F32),
            pltpu.VMEM((groups, width, points, LANES), F32),
            pltpu.VMEM((MANY, LANES, LANES), F32),
            pltpu.VMEM((MANY, LANES, LANES), F32),
            pltpu.VMEM((blocks, LANES), jnp.int32),
            pltpu.VMEM((LANES, blocks), jnp.int32),
            pltpu.SMEM((LANES, blocks), jnp.int32),
            pltpu.VMEM((rhs, 2, blocks * LANES), BF16),
            pltpu.SemaphoreType.DMA((levels + 3,)),
            pltpu.SemaphoreType.DMA((blocks // MANY,)),
        ],
        compiler_params=pltpu.CompilerParams(vmem_limit_bytes=36 << 20),
        name="target_fields",
    )(in_hbm(order), coef, in_vmem(head), in_hbm(factors), in_hbm(basis))


def local(
    sources,
    source_order,
    leaf_basis,
    leaf_ranks,
    source_factors,
    target_factors,
    target_basis,
    target_order,
):
    boxes, points, packed = leaf_basis.shape
    rhs, _, count = sources.shape
    groups = lax.axis_size("clu")
    per_group = boxes // groups
    order_in = source_order.reshape(count // LANES, LANES)
    order_out = target_order.reshape(count // LANES, LANES)
    basis = leaf_basis.reshape((groups, per_group) + leaf_basis.shape[1:])
    levels = source_factors.shape[0]
    factors = source_factors.reshape((levels, groups, per_group) + source_factors.shape[2:])
    target_w = target_factors.reshape((-1, groups, per_group) + target_factors.shape[2:])
    expansion = target_basis.reshape((groups, per_group) + target_basis.shape[1:])
    size = lax.axis_size("lvl")
    uppers = [
        (lax.axis_index("lvl") >> level & 1).reshape(1).astype(jnp.int32)
        for level in range(levels)
    ]
    outs = leaf_coefs(order_in, leaf_ranks, sources, basis, (factors,))
    coefs = list(outs[:PARTS])
    head = outs[PARTS]
    width = per_group // PARTS
    for level in range(levels):
        swap = [(i, i ^ 1 << level) for i in range(size)]
        last = level == levels - 1
        brought = []
        for k in range(PARTS):
            other = lax.ppermute(coefs[k], "lvl", swap)
            held, at = factors, k * width
            if level == 0:
                held = head
            elif last and k:
                held, at = brought[0], 0
            ahead = ()
            if last and k == 0:
                ahead = ((factors, level, width, per_group - width), (target_w, 0, 0, per_group))
            coefs[k], more = mix_level(
                uppers[level], coefs[k], other, held, level, at,
                resident=held is not factors, before=coefs[:k] if last else (), ahead=ahead,
            )
            brought += more
    coef = lax.all_to_all(coefs[-1], "clu", split_axis=0, concat_axis=0, tiled=True)
    return target_fields(order_out, coef, brought[1], target_w, expansion)


def solution(mesh):
    both = ("lvl", "clu")
    placed = (
        P(None, None, both),
        P(both, None),
        P(both, None, None),
        P(both),
        P(None, both, None, None, None),
        P(None, both, None, None, None),
        P(both, None, None),
        P(both, None),
    )
    return jax.shard_map(
        local, mesh=mesh, in_specs=placed, out_specs=P(None, None, both), check_vma=False
    )
```

time: 89.1 us -> 83.5 us (0.937)
  Pallas kernels: 46.9 us -> 41.6 us
    pallas_call x1, Pallas kernels: 17.8 us -> 14.9 us  [leaf_coefs(): pl.pallas_call(leaf_kernel, out_shape=[coef] * PARTS + [pltpu.VMEM(x.shap...]
    pallas_call x7, Pallas kernels: 29.2 us -> 26.6 us  [the longest x1 19 us: target_fields(): pl.pallas_call(target_kernel, out_shape=jax.ShapeDtypeStruct((rhs, 2, blo...]
  transfers between devices with their start and end apart: 6 -> 6, of which waited for: 4 -> 4; matrix products, arithmetic and copies ran while one was open for 0% -> 0% of each run, Pallas kernels for 8% -> 9%
where the time goes in v2:
time: 83.5 us; the launch traced here: 83.3 us
  Pallas kernels  41.6 us (50%)
  blocking collectives  18.7 us (22%)
  waiting for transfers between devices  13 us (16%)
  starting transfers between devices  9.88 us (12%)
    pallas_call x1, Pallas kernels, target_fields(): pl.pallas_call(target_kernel, out_shape=jax.ShapeDtypeStruct((rhs, 2, blo...  19 us
    all_to_all x1, blocking collectives, local(): lax.all_to_all(coefs[-1], 'clu', split_axis=0, concat_axis=0, tiled=True)  18.7 us
    pallas_call x1, Pallas kernels, leaf_coefs(): pl.pallas_call(leaf_kernel, out_shape=[coef] * PARTS + [pltpu.VMEM(x.shap...  14.9 us
    ppermute x6, waiting for transfers between devices, local(): other = lax.ppermute(coefs[k], 'lvl', swap)  13 us
    ppermute x6, starting transfers between devices, local(): other = lax.ppermute(coefs[k], 'lvl', swap)  9.88 us
    pallas_call x6, Pallas kernels, mix_level(): pl.pallas_call(functools.partial(mix_kernel, level, first, resident, len(...  7.65 us
  transfers between devices with their start and end apart: 6, of which 4 were waited for; matrix products, arithmetic and copies ran while one was open for 0% of the time, Pallas kernels for 9%

profile of v2, /device:TPU:0, one launch (start us, length us, event | category | flops | bytes accessed | tf_op | source)
XLA Modules:
  0.0 83.3 jit_solution(13007817112408834438)
XLA Ops:
  0.0 14.9 %leaf_coefs.1 = (bf16[16,2,32,128]{3,2,1,0:T(8,128)(2,1)S(1)}, bf16[16,2,32,128]{3,2,1,0:T(8,128)(2,1)S(1)}, bf16[16,4,2,64,128]{4,3,2,1,0:T(8,128)(2,1)S(1)}) custom-call(s32[128,128]{1,0:T(8,128)} %bitcast.18, s32[64]{0:T(128)} %ranks_hbm.1, bf16[32,2,16384]{2,1,0:T(2,128)(2,1)} %source_hbm.1, bf16[16,4,256,128]{3,2,1,0:T(8,128)(2,1)} %bitcast.16, ...), custom_call_target="tpu_custom_call" | custom-call | tf_op jit(solution)/shard_map/leaf_coefs/pallas_call | solution.py:158
  14.9 0.1 collective-permute-start.3
  15.0 0.5 collective-permute-start
  15.5 1.0 %collective-permute-done.3.other_ref = bf16[16,2,32,128]{3,2,1,0:T(8,128)(2,1)S(1)} collective-permute-done((bf16[16,2,32,128]{3,2,1,0:T(8,128)(2,1)S(1)}, bf16[16,2,32,128]{3,2,1,0:T(8,128)(2,1)S(1)}, u32[]{:S(2)}, u32[]{:S(2)}) %collective-permute-start.3) | collective-permute-done | bytes 262176 | tf_op jit(solution)/shard_map/ppermute | solution.py:417
  16.6 0.6 mix_level.8.own_ref
  17.1 1.7 %collective-permute-start.4 = (bf16[16,2,32,128]{3,2,1,0:T(8,128)(2,1)S(1)}, bf16[16,2,32,128]{3,2,1,0:T(8,128)(2,1)S(1)}, u32[]{:S(2)}, u32[]{:S(2)}) collective-permute-start(bf16[16,2,32,128]{3,2,1,0:T(8,128)(2,1)S(1)} %mix_level.8.own_ref), channel_id=1, source_target_pairs={{0,32},{16,48},{32,0},{48,16},{64,96},{80,112},{96,64},{112,80},{1... | collective-permute-start | bytes 786440 | tf_op jit(solution)/shard_map/ppermute | solution.py:417
  18.9 0.0 collective-permute-done.other_ref
  18.9 0.6 mix_level.6.own_ref
  19.4 0.4 collective-permute-start.1
  19.9 6.5 %collective-permute-done.4.other_ref = bf16[16,2,32,128]{3,2,1,0:T(8,128)(2,1)S(1)} collective-permute-done((bf16[16,2,32,128]{3,2,1,0:T(8,128)(2,1)S(1)}, bf16[16,2,32,128]{3,2,1,0:T(8,128)(2,1)S(1)}, u32[]{:S(2)}, u32[]{:S(2)}) %collective-permute-start.4) | collective-permute-done | bytes 262176 | tf_op jit(solution)/shard_map/ppermute | solution.py:417
  26.4 1.9 %mix_level.9.own_ref = bf16[16,2,32,128]{3,2,1,0:T(8,128)(2,1)S(1)} custom-call(s32[1]{0:T(128)} %bitcast.2.upper_ref, bf16[16,2,32,128]{3,2,1,0:T(8,128)(2,1)S(1)} %mix_level.8.own_ref, bf16[16,2,32,128]{3,2,1,0:T(8,128)(2,1)S(1)} %collective-permute-done.4.other_ref, bf16[3,16,4,2,64,128]{5,4,3,2,1,0:T(8,128)(2,1)} %bitcast.10), custom_call_target="tpu_custom_call" | custom-call | tf_op jit(solution)/shard_map/mix_level/pallas_call | solution.py:234
  28.2 3.4 %collective-permute-start.5 = (bf16[16,2,32,128]{3,2,1,0:T(8,128)(2,1)S(1)}, bf16[16,2,32,128]{3,2,1,0:T(8,128)(2,1)S(1)}, u32[]{:S(2)}, u32[]{:S(2)}) collective-permute-start(bf16[16,2,32,128]{3,2,1,0:T(8,128)(2,1)S(1)} %mix_level.9.own_ref), channel_id=1, source_target_pairs={{0,64},{16,80},{32,96},{48,112},{64,0},{80,16},{96,32},{112,48},{1... | collective-permute-start | bytes 786440 | tf_op jit(solution)/shard_map/ppermute | solution.py:417
  31.6 0.0 collective-permute-done.1.other_ref
  31.6 1.9 %mix_level.7.own_ref = bf16[16,2,32,128]{3,2,1,0:T(8,128)(2,1)S(1)} custom-call(s32[1]{0:T(128)} %bitcast.2.upper_ref, bf16[16,2,32,128]{3,2,1,0:T(8,128)(2,1)S(1)} %mix_level.6.own_ref, bf16[16,2,32,128]{3,2,1,0:T(8,128)(2,1)S(1)} %collective-permute-done.1.other_ref, bf16[3,16,4,2,64,128]{5,4,3,2,1,0:T(8,128)(2,1)} %bitcast.11), custom_call_target="tpu_custom_call" | custom-call | tf_op jit(solution)/shard_map/mix_level/pallas_call | solution.py:234
  33.4 3.8 %collective-permute-start.2 = (bf16[16,2,32,128]{3,2,1,0:T(8,128)(2,1)S(1)}, bf16[16,2,32,128]{3,2,1,0:T(8,128)(2,1)S(1)}, u32[]{:S(2)}, u32[]{:S(2)}) collective-permute-start(bf16[16,2,32,128]{3,2,1,0:T(8,128)(2,1)S(1)} %mix_level.7.own_ref), channel_id=1, source_target_pairs={{0,64},{16,80},{32,96},{48,112},{64,0},{80,16},{96,32},{112,48},{1... | collective-permute-start | bytes 786440 | tf_op jit(solution)/shard_map/ppermute | solution.py:417
  37.2 2.9 %collective-permute-done.5.other_ref = bf16[16,2,32,128]{3,2,1,0:T(8,128)(2,1)S(1)} collective-permute-done((bf16[16,2,32,128]{3,2,1,0:T(8,128)(2,1)S(1)}, bf16[16,2,32,128]{3,2,1,0:T(8,128)(2,1)S(1)}, u32[]{:S(2)}, u32[]{:S(2)}) %collective-permute-start.5) | collective-permute-done | bytes 262176 | tf_op jit(solution)/shard_map/ppermute | solution.py:417
  40.1 2.3 %mix_level.10 = (bf16[16,2,32,128]{3,2,1,0:T(8,128)(2,1)S(1)}, bf16[16,2,2,64,128]{4,3,2,1,0:T(8,128)(2,1)S(1)}, bf16[16,4,2,64,128]{4,3,2,1,0:T(8,128)(2,1)S(1)}) custom-call(s32[1]{0:T(128)} %bitcast.1.upper_ref, bf16[16,2,32,128]{3,2,1,0:T(8,128)(2,1)S(1)} %mix_level.9.own_ref, bf16[16,2,32,128]{3,2,1,0:T(8,128)(2,1)S(1)} %collective-permute-done.5.other_ref, ...), custom_call_target="tpu_custom_call" | custom-call | tf_op jit(solution)/shard_map/mix_level/pallas_call | solution.py:234
  42.4 2.5 %collective-permute-done.2.other_ref = bf16[16,2,32,128]{3,2,1,0:T(8,128)(2,1)S(1)} collective-permute-done((bf16[16,2,32,128]{3,2,1,0:T(8,128)(2,1)S(1)}, bf16[16,2,32,128]{3,2,1,0:T(8,128)(2,1)S(1)}, u32[]{:S(2)}, u32[]{:S(2)}) %collective-permute-start.2) | collective-permute-done | bytes 262176 | tf_op jit(solution)/shard_map/ppermute | solution.py:417
  44.9 0.6 mix_level.11
  45.5 18.7 %all_to_all.5.coef_ref = bf16[16,4,32,128]{3,2,1,0:T(8,128)(2,1)S(1)} all-to-all(bf16[16,4,32,128]{3,2,1,0:T(8,128)(2,1)S(1)} %mix_level.11), channel_id=1, replica_groups=mesh['lvl'=8,'clu'=16] {'clu'}, dimensions={0} | all-to-all | bytes 1048576 | tf_op jit(solution)/shard_map/all_to_all | solution.py:431
  64.2 19.0 %target_fields.1 = bf16[32,2,16384]{2,1,0:T(2,128)(2,1)} custom-call(s32[128,128]{1,0:T(8,128)} %bitcast.19, bf16[16,4,32,128]{3,2,1,0:T(8,128)(2,1)S(1)} %all_to_all.5.coef_ref, bf16[16,4,2,64,128]{4,3,2,1,0:T(8,128)(2,1)S(1)} %get-tuple-element.16.head, bf16[4,16,4,2,64,128]{5,4,3,2,1,0:T(8,128)(2,1)} %bitcast.15, bf16[16,4,64,512]{3,2,1,0:T(8,128)(2,1)} %bitcast.17), custom_call_target="tpu_custom_call" | custom-call | tf_op jit(solution)/shard_map/target_fields/pallas_call | solution.py:357
Async XLA Ops:
  14.9 1.6 %collective-permute-start.3 = (bf16[16,2,32,128]{3,2,1,0:T(8,128)(2,1)S(1)}, bf16[16,2,32,128]{3,2,1,0:T(8,128)(2,1)S(1)}, u32[]{:S(2)}, u32[]{:S(2)}) collective-permute-start(bf16[16,2,32,128]{3,2,1,0:T(8,128)(2,1)S(1)} %get-tuple-element.13.own_ref), channel_id=1, source_target_pairs={{0,16},{16,0},{32,48},{48,32},{64,80},{80,64},{96,112},{112,96},{1... | collective-permute-start | bytes 786440 | tf_op jit(solution)/shard_map/ppermute | solution.py:417
  15.0 3.8 %collective-permute-start = (bf16[16,2,32,128]{3,2,1,0:T(8,128)(2,1)S(1)}, bf16[16,2,32,128]{3,2,1,0:T(8,128)(2,1)S(1)}, u32[]{:S(2)}, u32[]{:S(2)}) collective-permute-start(bf16[16,2,32,128]{3,2,1,0:T(8,128)(2,1)S(1)} %get-tuple-element.11.own_ref), channel_id=1, source_target_pairs={{0,16},{16,0},{32,48},{48,32},{64,80},{80,64},{96,112},{112,96},{1... | collective-permute-start | bytes 786440 | tf_op jit(solution)/shard_map/ppermute | solution.py:417
  17.1 9.2 %collective-permute-start.4 = (bf16[16,2,32,128]{3,2,1,0:T(8,128)(2,1)S(1)}, bf16[16,2,32,128]{3,2,1,0:T(8,128)(2,1)S(1)}, u32[]{:S(2)}, u32[]{:S(2)}) collective-permute-start(bf16[16,2,32,128]{3,2,1,0:T(8,128)(2,1)S(1)} %mix_level.8.own_ref), channel_id=1, source_target_pairs={{0,32},{16,48},{32,0},{48,16},{64,96},{80,112},{96,64},{112,80},{1... | collective-permute-start | bytes 786440 | tf_op jit(solution)/shard_map/ppermute | solution.py:417
  19.4 12.1 %collective-permute-start.1 = (bf16[16,2,32,128]{3,2,1,0:T(8,128)(2,1)S(1)}, bf16[16,2,32,128]{3,2,1,0:T(8,128)(2,1)S(1)}, u32[]{:S(2)}, u32[]{:S(2)}) collective-permute-start(bf16[16,2,32,128]{3,2,1,0:T(8,128)(2,1)S(1)} %mix_level.6.own_ref), channel_id=1, source_target_pairs={{0,32},{16,48},{32,0},{48,16},{64,96},{80,112},{96,64},{112,80},{1... | collective-permute-start | bytes 786440 | tf_op jit(solution)/shard_map/ppermute | solution.py:417
  28.2 11.9 %collective-permute-start.5 = (bf16[16,2,32,128]{3,2,1,0:T(8,128)(2,1)S(1)}, bf16[16,2,32,128]{3,2,1,0:T(8,128)(2,1)S(1)}, u32[]{:S(2)}, u32[]{:S(2)}) collective-permute-start(bf16[16,2,32,128]{3,2,1,0:T(8,128)(2,1)S(1)} %mix_level.9.own_ref), channel_id=1, source_target_pairs={{0,64},{16,80},{32,96},{48,112},{64,0},{80,16},{96,32},{112,48},{1... | collective-permute-start | bytes 786440 | tf_op jit(solution)/shard_map/ppermute | solution.py:417
  33.4 11.5 %collective-permute-start.2 = (bf16[16,2,32,128]{3,2,1,0:T(8,128)(2,1)S(1)}, bf16[16,2,32,128]{3,2,1,0:T(8,128)(2,1)S(1)}, u32[]{:S(2)}, u32[]{:S(2)}) collective-permute-start(bf16[16,2,32,128]{3,2,1,0:T(8,128)(2,1)S(1)} %mix_level.7.own_ref), channel_id=1, source_target_pairs={{0,64},{16,80},{32,96},{48,112},{64,0},{80,16},{96,32},{112,48},{1... | collective-permute-start | bytes 786440 | tf_op jit(solution)/shard_map/ppermute | solution.py:417

commit v3 on v2

--- a/solution.py
+++ b/solution.py
@@ -92,7 +92,7 @@
     coef_refs, refs = refs[:PARTS], refs[PARTS:]
     loads_ref, refs = refs[:EXTRA], refs[EXTRA:]
     table, turned, source, basis, held, mixed, order_vmem, order, ranks, sems = refs
-    rhs, _, count = source.shape
+    rhs, _, count = source_hbm.shape
     columns = 2 * rhs
     pieces = 4
     cut = count // pieces
@@ -163,7 +163,7 @@
         scratch_shapes=[
             pltpu.VMEM((count, LANES), F32),
             pltpu.VMEM((LANES, segments), jnp.int32),
-            pltpu.VMEM(source.shape, BF16),
+            pltpu.VMEM((rhs, 2, count + LANES), BF16),
             pltpu.VMEM(basis.shape, BF16),
             pltpu.VMEM((groups, width, points, LANES), F32),
             pltpu.VMEM((BATCH, width, 2 * rhs, packed), F32),
@@ -370,7 +370,7 @@
             pltpu.VMEM((blocks, LANES), jnp.int32),
             pltpu.VMEM((LANES, blocks), jnp.int32),
             pltpu.SMEM((LANES, blocks), jnp.int32),
-            pltpu.VMEM((rhs, 2, blocks * LANES), BF16),
+            pltpu.VMEM((rhs, 2, (blocks + 1) * LANES), BF16),
             pltpu.SemaphoreType.DMA((levels + 3,)),
             pltpu.SemaphoreType.DMA((blocks // MANY,)),
         ],
@@ -418,9 +418,13 @@
             held, at = factors, k * width
             if level == 0:
                 held = head
+            elif level == 1 and k == 0:
+                held, at = early[0], 0
             elif last and k:
                 held, at = brought[0], 0
             ahead = ()
+            if level == 0 and k == PARTS - 1:
+                ahead = ((factors, 1, 0, width),)
             if last and k == 0:
                 ahead = ((factors, level, width, per_group - width), (target_w, 0, 0, per_group))
             coefs[k], more = mix_level(
@@ -428,6 +432,8 @@
                 resident=held is not factors, before=coefs[:k] if last else (), ahead=ahead,
             )
             brought += more
+        if level == 0:
+            early = brought
     coef = lax.all_to_all(coefs[-1], "clu", split_axis=0, concat_axis=0, tiled=True)
     return target_fields(order_out, coef, brought[1], target_w, expansion)
 

time: 83.5 us -> 81.3 us (0.974)
  waiting for transfers between devices: 13 us -> 8.66 us
  local copies, waits for them, and re-layouts: 0 us -> 2.62 us
    ppermute x6, waiting for transfers between devices: 13 us -> 8.66 us  [local(): other = lax.ppermute(coefs[k], 'lvl', swap)]
    unnamed x0 -> x8, local copies, waits for them, and re-layouts: none -> 2.62 us
    pallas_call x6, Pallas kernels: 7.65 us -> 9.85 us  [mix_level(): pl.pallas_call(functools.partial(mix_kernel, level, first, resident, len(...]
    pallas_call x1, Pallas kernels: 14.9 us -> 13.8 us  [leaf_coefs(): pl.pallas_call(leaf_kernel, out_shape=[coef] * PARTS + [pltpu.VMEM(x.shap...]
  transfers between devices with their start and end apart: 6 -> 6, of which waited for: 4 -> 5; matrix products, arithmetic and copies ran while one was open for 0% -> 0% of each run, Pallas kernels for 9% -> 11%
where the time goes in v3:
time: 81.3 us; the launch traced here: 81 us
  Pallas kernels  42.1 us (52%)
  blocking collectives  18 us (22%)
  starting transfers between devices  9.37 us (12%)
  waiting for transfers between devices  8.66 us (11%)
  local copies, waits for them, and re-layouts  2.62 us (3%)
    pallas_call x1, Pallas kernels, target_fields(): pl.pallas_call(target_kernel, out_shape=jax.ShapeDtypeStruct((rhs, 2, blo...  18.5 us
    all_to_all x1, blocking collectives, local(): lax.all_to_all(coefs[-1], 'clu', split_axis=0, concat_axis=0, tiled=True)  18 us
    pallas_call x1, Pallas kernels, leaf_coefs(): pl.pallas_call(leaf_kernel, out_shape=[coef] * PARTS + [pltpu.VMEM(x.shap...  13.8 us
    pallas_call x6, Pallas kernels, mix_level(): pl.pallas_call(functools.partial(mix_kernel, level, first, resident, len(...  9.85 us
    ppermute x6, starting transfers between devices, local(): other = lax.ppermute(coefs[k], 'lvl', swap)  9.37 us
    ppermute x6, waiting for transfers between devices, local(): other = lax.ppermute(coefs[k], 'lvl', swap)  8.66 us
    unnamed x8, local copies, waits for them, and re-layouts  2.62 us
  transfers between devices with their start and end apart: 6, of which 5 were waited for; matrix products, arithmetic and copies ran while one was open for 0% of the time, Pallas kernels for 11%

profile of v3, /device:TPU:0, one launch (start us, length us, event | category | flops | bytes accessed | tf_op | source)
XLA Modules:
  0.0 81.0 jit_solution(8147941314313904027)
XLA Ops:
  0.0 13.8 %leaf_coefs.1 = (bf16[16,2,32,128]{3,2,1,0:T(8,128)(2,1)S(1)}, bf16[16,2,32,128]{3,2,1,0:T(8,128)(2,1)S(1)}, bf16[16,4,2,64,128]{4,3,2,1,0:T(8,128)(2,1)S(1)}) custom-call(s32[128,128]{1,0:T(8,128)} %bitcast.18, s32[64]{0:T(128)} %ranks_hbm.1, bf16[32,2,16384]{2,1,0:T(2,128)(2,1)} %source_hbm.1, bf16[16,4,256,128]{3,2,1,0:T(8,128)(2,1)} %bitcast.16, ...), custom_call_target="tpu_custom_call" | custom-call | tf_op jit(solution)/shard_map/leaf_coefs/pallas_call | solution.py:158
  13.8 0.0 copy-start
  13.8 0.1 collective-permute-start.3
  13.9 0.5 collective-permute-start
  14.4 1.0 %collective-permute-done.3.other_ref = bf16[16,2,32,128]{3,2,1,0:T(8,128)(2,1)S(1)} collective-permute-done((bf16[16,2,32,128]{3,2,1,0:T(8,128)(2,1)S(1)}, bf16[16,2,32,128]{3,2,1,0:T(8,128)(2,1)S(1)}, u32[]{:S(2)}, u32[]{:S(2)}) %collective-permute-start.3) | collective-permute-done | bytes 262176 | tf_op jit(solution)/shard_map/ppermute | solution.py:417
  15.5 0.6 mix_level.8.own_ref
  16.0 1.7 %collective-permute-start.4 = (bf16[16,2,32,128]{3,2,1,0:T(8,128)(2,1)S(1)}, bf16[16,2,32,128]{3,2,1,0:T(8,128)(2,1)}, u32[]{:S(2)}, u32[]{:S(2)}) collective-permute-start(bf16[16,2,32,128]{3,2,1,0:T(8,128)(2,1)S(1)} %mix_level.8.own_ref), channel_id=1, source_target_pairs={{0,32},{16,48},{32,0},{48,16},{64,96},{80,112},{96,64},{112,80},{1... | collective-permute-start | bytes 786440 | tf_op jit(solution)/shard_map/ppermute | solution.py:417
  17.8 0.7 copy-done.2
  18.5 0.9 %copy-done.1 = bf16[16,2,32,128]{3,2,1,0:T(8,128)(2,1)S(1)} copy-done((bf16[16,2,32,128]{3,2,1,0:T(8,128)(2,1)S(1)}, bf16[16,2,32,128]{3,2,1,0:T(8,128)(2,1)}, u32[]{:S(2)}) %copy-start.1) | copy-done | bytes 262168
  19.4 0.9 %copy-done.3 = bf16[16,2,32,128]{3,2,1,0:T(8,128)(2,1)S(1)} copy-done((bf16[16,2,32,128]{3,2,1,0:T(8,128)(2,1)S(1)}, bf16[16,2,32,128]{3,2,1,0:T(8,128)(2,1)}, u32[]{:S(2)}) %copy-start.3) | copy-done | bytes 262168
  20.4 2.2 %mix_level.6 = (bf16[16,2,32,128]{3,2,1,0:T(8,128)(2,1)}, bf16[16,2,2,64,128]{4,3,2,1,0:T(8,128)(2,1)S(1)}) custom-call(s32[1]{0:T(128)} %bitcast.3.upper_ref, bf16[16,2,32,128]{3,2,1,0:T(8,128)(2,1)S(1)} %copy-done.1, bf16[16,2,32,128]{3,2,1,0:T(8,128)(2,1)S(1)} %copy-done.3, bf16[16,4,2,64,128]{4,3,2,1,0:T(8,128)(2,1)S(1)} %get-tuple-element.14.factor_ref, ...), custom_call_target="tpu_custom_call" | custom-call | tf_op jit(solution)/shard_map/mix_level/pallas_call | solution.py:234
  22.6 0.4 collective-permute-start.1
  23.0 1.6 %collective-permute-done.4.other_ref = bf16[16,2,32,128]{3,2,1,0:T(8,128)(2,1)} collective-permute-done((bf16[16,2,32,128]{3,2,1,0:T(8,128)(2,1)S(1)}, bf16[16,2,32,128]{3,2,1,0:T(8,128)(2,1)}, u32[]{:S(2)}, u32[]{:S(2)}) %collective-permute-start.4) | collective-permute-done | bytes 262176 | tf_op jit(solution)/shard_map/ppermute | solution.py:417
  24.6 1.5 %mix_level.9.own_ref = bf16[16,2,32,128]{3,2,1,0:T(8,128)(2,1)S(1)} custom-call(s32[1]{0:T(128)} %bitcast.2.upper_ref, bf16[16,2,32,128]{3,2,1,0:T(8,128)(2,1)S(1)} %mix_level.8.own_ref, bf16[16,2,32,128]{3,2,1,0:T(8,128)(2,1)} %collective-permute-done.4.other_ref, bf16[16,2,2,64,128]{4,3,2,1,0:T(8,128)(2,1)S(1)} %get-tuple-element.17.factor_ref), custom_call_target="tpu_custom_call" | custom-call | tf_op jit(solution)/shard_map/mix_level/pallas_call | solution.py:234
  26.1 3.4 %collective-permute-start.5 = (bf16[16,2,32,128]{3,2,1,0:T(8,128)(2,1)S(1)}, bf16[16,2,32,128]{3,2,1,0:T(8,128)(2,1)S(1)}, u32[]{:S(2)}, u32[]{:S(2)}) collective-permute-start(bf16[16,2,32,128]{3,2,1,0:T(8,128)(2,1)S(1)} %mix_level.9.own_ref), channel_id=1, source_target_pairs={{0,64},{16,80},{32,96},{48,112},{64,0},{80,16},{96,32},{112,48},{1... | collective-permute-start | bytes 786440 | tf_op jit(solution)/shard_map/ppermute | solution.py:417
  29.4 2.3 %collective-permute-done.1.other_ref = bf16[16,2,32,128]{3,2,1,0:T(8,128)(2,1)S(1)} collective-permute-done((bf16[16,2,32,128]{3,2,1,0:T(8,128)(2,1)}, bf16[16,2,32,128]{3,2,1,0:T(8,128)(2,1)S(1)}, u32[]{:S(2)}, u32[]{:S(2)}) %collective-permute-start.1) | collective-permute-done | bytes 262176 | tf_op jit(solution)/shard_map/ppermute | solution.py:417
  31.8 2.8 %mix_level.7.own_ref = bf16[16,2,32,128]{3,2,1,0:T(8,128)(2,1)S(1)} custom-call(s32[1]{0:T(128)} %bitcast.2.upper_ref, bf16[16,2,32,128]{3,2,1,0:T(8,128)(2,1)} %get-tuple-element.15.own_ref, bf16[16,2,32,128]{3,2,1,0:T(8,128)(2,1)S(1)} %collective-permute-done.1.other_ref, bf16[3,16,4,2,64,128]{5,4,3,2,1,0:T(8,128)(2,1)} %bitcast.11), custom_call_target="tpu_custom_call" | custom-call | tf_op jit(solution)/shard_map/mix_level/pallas_call | solution.py:234
  34.6 3.2 %collective-permute-start.2 = (bf16[16,2,32,128]{3,2,1,0:T(8,128)(2,1)S(1)}, bf16[16,2,32,128]{3,2,1,0:T(8,128)(2,1)S(1)}, u32[]{:S(2)}, u32[]{:S(2)}) collective-permute-start(bf16[16,2,32,128]{3,2,1,0:T(8,128)(2,1)S(1)} %mix_level.7.own_ref), channel_id=1, source_target_pairs={{0,64},{16,80},{32,96},{48,112},{64,0},{80,16},{96,32},{112,48},{1... | collective-permute-start | bytes 786440 | tf_op jit(solution)/shard_map/ppermute | solution.py:417
  37.8 1.4 %collective-permute-done.5.other_ref = bf16[16,2,32,128]{3,2,1,0:T(8,128)(2,1)S(1)} collective-permute-done((bf16[16,2,32,128]{3,2,1,0:T(8,128)(2,1)S(1)}, bf16[16,2,32,128]{3,2,1,0:T(8,128)(2,1)S(1)}, u32[]{:S(2)}, u32[]{:S(2)}) %collective-permute-start.5) | collective-permute-done | bytes 262176 | tf_op jit(solution)/shard_map/ppermute | solution.py:417
  39.3 2.3 %mix_level.10 = (bf16[16,2,32,128]{3,2,1,0:T(8,128)(2,1)S(1)}, bf16[16,2,2,64,128]{4,3,2,1,0:T(8,128)(2,1)S(1)}, bf16[16,4,2,64,128]{4,3,2,1,0:T(8,128)(2,1)S(1)}) custom-call(s32[1]{0:T(128)} %bitcast.1.upper_ref, bf16[16,2,32,128]{3,2,1,0:T(8,128)(2,1)S(1)} %mix_level.9.own_ref, bf16[16,2,32,128]{3,2,1,0:T(8,128)(2,1)S(1)} %collective-permute-done.5.other_ref, ...), custom_call_target="tpu_custom_call" | custom-call | tf_op jit(solution)/shard_map/mix_level/pallas_call | solution.py:234
  41.5 2.3 %collective-permute-done.2.other_ref = bf16[16,2,32,128]{3,2,1,0:T(8,128)(2,1)S(1)} collective-permute-done((bf16[16,2,32,128]{3,2,1,0:T(8,128)(2,1)S(1)}, bf16[16,2,32,128]{3,2,1,0:T(8,128)(2,1)S(1)}, u32[]{:S(2)}, u32[]{:S(2)}) %collective-permute-start.2) | collective-permute-done | bytes 262176 | tf_op jit(solution)/shard_map/ppermute | solution.py:417
  43.8 0.6 mix_level.11
  44.4 18.0 %all_to_all.5.coef_ref = bf16[16,4,32,128]{3,2,1,0:T(8,128)(2,1)S(1)} all-to-all(bf16[16,4,32,128]{3,2,1,0:T(8,128)(2,1)S(1)} %mix_level.11), channel_id=1, replica_groups=mesh['lvl'=8,'clu'=16] {'clu'}, dimensions={0} | all-to-all | bytes 1048576 | tf_op jit(solution)/shard_map/all_to_all | solution.py:437
  62.4 18.5 %target_fields.1 = bf16[32,2,16384]{2,1,0:T(2,128)(2,1)} custom-call(s32[128,128]{1,0:T(8,128)} %bitcast.19, bf16[16,4,32,128]{3,2,1,0:T(8,128)(2,1)S(1)} %all_to_all.5.coef_ref, bf16[16,4,2,64,128]{4,3,2,1,0:T(8,128)(2,1)S(1)} %get-tuple-element.20.head, bf16[4,16,4,2,64,128]{5,4,3,2,1,0:T(8,128)(2,1)} %bitcast.15, bf16[16,4,64,512]{3,2,1,0:T(8,128)(2,1)} %bitcast.17), custom_call_target="tpu_custom_call" | custom-call | tf_op jit(solution)/shard_map/target_fields/pallas_call | solution.py:357
  (5 shorter events, 0.0 us)
Async XLA Ops:
  13.8 3.9 %copy-start = (bf16[16,2,32,128]{3,2,1,0:T(8,128)(2,1)}, bf16[16,2,32,128]{3,2,1,0:T(8,128)(2,1)S(1)}, u32[]{:S(2)}) copy-start(bf16[16,2,32,128]{3,2,1,0:T(8,128)(2,1)S(1)} %get-tuple-element.13.own_ref) | copy-start | bytes 786436
  13.8 1.6 %collective-permute-start.3 = (bf16[16,2,32,128]{3,2,1,0:T(8,128)(2,1)S(1)}, bf16[16,2,32,128]{3,2,1,0:T(8,128)(2,1)S(1)}, u32[]{:S(2)}, u32[]{:S(2)}) collective-permute-start(bf16[16,2,32,128]{3,2,1,0:T(8,128)(2,1)S(1)} %get-tuple-element.16.own_ref), channel_id=1, source_target_pairs={{0,16},{16,0},{32,48},{48,32},{64,80},{80,64},{96,112},{112,96},{1... | collective-permute-start | bytes 786440 | tf_op jit(solution)/shard_map/ppermute | solution.py:417
  13.9 3.8 %collective-permute-start = (bf16[16,2,32,128]{3,2,1,0:T(8,128)(2,1)S(1)}, bf16[16,2,32,128]{3,2,1,0:T(8,128)(2,1)S(1)}, u32[]{:S(2)}, u32[]{:S(2)}) collective-permute-start(bf16[16,2,32,128]{3,2,1,0:T(8,128)(2,1)S(1)} %get-tuple-element.13.own_ref), channel_id=1, source_target_pairs={{0,16},{16,0},{32,48},{48,32},{64,80},{80,64},{96,112},{112,96},{1... | collective-permute-start | bytes 786440 | tf_op jit(solution)/shard_map/ppermute | solution.py:417
  16.0 8.5 %collective-permute-start.4 = (bf16[16,2,32,128]{3,2,1,0:T(8,128)(2,1)S(1)}, bf16[16,2,32,128]{3,2,1,0:T(8,128)(2,1)}, u32[]{:S(2)}, u32[]{:S(2)}) collective-permute-start(bf16[16,2,32,128]{3,2,1,0:T(8,128)(2,1)S(1)} %mix_level.8.own_ref), channel_id=1, source_target_pairs={{0,32},{16,48},{32,0},{48,16},{64,96},{80,112},{96,64},{112,80},{1... | collective-permute-start | bytes 786440 | tf_op jit(solution)/shard_map/ppermute | solution.py:417
  17.8 0.7 copy-start.2
  18.5 0.9 %copy-start.1 = (bf16[16,2,32,128]{3,2,1,0:T(8,128)(2,1)S(1)}, bf16[16,2,32,128]{3,2,1,0:T(8,128)(2,1)}, u32[]{:S(2)}) copy-start(bf16[16,2,32,128]{3,2,1,0:T(8,128)(2,1)} %copy-done) | copy-start | bytes 786436
  19.4 0.9 %copy-start.3 = (bf16[16,2,32,128]{3,2,1,0:T(8,128)(2,1)S(1)}, bf16[16,2,32,128]{3,2,1,0:T(8,128)(2,1)}, u32[]{:S(2)}) copy-start(bf16[16,2,32,128]{3,2,1,0:T(8,128)(2,1)} %copy-done.2) | copy-start | bytes 786436
  22.6 9.2 %collective-permute-start.1 = (bf16[16,2,32,128]{3,2,1,0:T(8,128)(2,1)}, bf16[16,2,32,128]{3,2,1,0:T(8,128)(2,1)S(1)}, u32[]{:S(2)}, u32[]{:S(2)}) collective-permute-start(bf16[16,2,32,128]{3,2,1,0:T(8,128)(2,1)} %get-tuple-element.15.own_ref), channel_id=1, source_target_pairs={{0,32},{16,48},{32,0},{48,16},{64,96},{80,112},{96,64},{112,80},{1... | collective-permute-start | bytes 786440 | tf_op jit(solution)/shard_map/ppermute | solution.py:417
  26.1 13.2 %collective-permute-start.5 = (bf16[16,2,32,128]{3,2,1,0:T(8,128)(2,1)S(1)}, bf16[16,2,32,128]{3,2,1,0:T(8,128)(2,1)S(1)}, u32[]{:S(2)}, u32[]{:S(2)}) collective-permute-start(bf16[16,2,32,128]{3,2,1,0:T(8,128)(2,1)S(1)} %mix_level.9.own_ref), channel_id=1, source_target_pairs={{0,64},{16,80},{32,96},{48,112},{64,0},{80,16},{96,32},{112,48},{1... | collective-permute-start | bytes 786440 | tf_op jit(solution)/shard_map/ppermute | solution.py:417
  34.6 9.3 %collective-permute-start.2 = (bf16[16,2,32,128]{3,2,1,0:T(8,128)(2,1)S(1)}, bf16[16,2,32,128]{3,2,1,0:T(8,128)(2,1)S(1)}, u32[]{:S(2)}, u32[]{:S(2)}) collective-permute-start(bf16[16,2,32,128]{3,2,1,0:T(8,128)(2,1)S(1)} %mix_level.7.own_ref), channel_id=1, source_target_pairs={{0,64},{16,80},{32,96},{48,112},{64,0},{80,16},{96,32},{112,48},{1... | collective-permute-start | bytes 786440 | tf_op jit(solution)/shard_map/ppermute | solution.py:417

commit v4 on v3

--- a/solution.py
+++ b/solution.py
@@ -11,11 +11,11 @@
 BF16 = jnp.bfloat16
 LANES = 128
 PER_GROUP = 4
-MANY = 8
+MANY = 16
 PARTS = 2
 EXTRA = 1
 LEAF_LIMIT = 32
-BATCH = 8
+BATCH = 16
 
 
 def lane_halves(shape):

time: 81.3 us -> 80.8 us (level)
  transfers between devices with their start and end apart: 6 -> 6, of which waited for: 5 -> 5; matrix products, arithmetic and copies ran while one was open for 0% -> 0% of each run, Pallas kernels for 11% -> 12%
where the time goes in v4:
time: 80.8 us; the launch traced here: 80.5 us
  Pallas kernels  41.7 us (52%)
  blocking collectives  18 us (22%)
  starting transfers between devices  9.37 us (12%)
  waiting for transfers between devices  8.66 us (11%)
  local copies, waits for them, and re-layouts  2.62 us (3%)
    pallas_call x1, Pallas kernels, target_fields(): pl.pallas_call(target_kernel, out_shape=jax.ShapeDtypeStruct((rhs, 2, blo...  18.2 us
    all_to_all x1, blocking collectives, local(): lax.all_to_all(coefs[-1], 'clu', split_axis=0, concat_axis=0, tiled=True)  18 us
    pallas_call x1, Pallas kernels, leaf_coefs(): pl.pallas_call(leaf_kernel, out_shape=[coef] * PARTS + [pltpu.VMEM(x.shap...  13.6 us
    pallas_call x6, Pallas kernels, mix_level(): pl.pallas_call(functools.partial(mix_kernel, level, first, resident, len(...  9.85 us
    ppermute x6, starting transfers between devices, local(): other = lax.ppermute(coefs[k], 'lvl', swap)  9.37 us
    ppermute x6, waiting for transfers between devices, local(): other = lax.ppermute(coefs[k], 'lvl', swap)  8.66 us
    unnamed x8, local copies, waits for them, and re-layouts  2.62 us
  transfers between devices with their start and end apart: 6, of which 5 were waited for; matrix products, arithmetic and copies ran while one was open for 0% of the time, Pallas kernels for 12%

profile of v4, /device:TPU:0, one launch (start us, length us, event | category | flops | bytes accessed | tf_op | source)
XLA Modules:
  0.0 80.5 jit_solution(11572143097580891889)
XLA Ops:
  0.0 13.6 %leaf_coefs.1 = (bf16[16,2,32,128]{3,2,1,0:T(8,128)(2,1)S(1)}, bf16[16,2,32,128]{3,2,1,0:T(8,128)(2,1)S(1)}, bf16[16,4,2,64,128]{4,3,2,1,0:T(8,128)(2,1)S(1)}) custom-call(s32[128,128]{1,0:T(8,128)} %bitcast.18, s32[64]{0:T(128)} %ranks_hbm.1, bf16[32,2,16384]{2,1,0:T(2,128)(2,1)} %source_hbm.1, bf16[16,4,256,128]{3,2,1,0:T(8,128)(2,1)} %bitcast.16, ...), custom_call_target="tpu_custom_call" | custom-call | tf_op jit(solution)/shard_map/leaf_coefs/pallas_call | solution.py:158
  13.6 0.0 copy-start
  13.6 0.1 collective-permute-start.3
  13.7 0.5 collective-permute-start
  14.2 1.0 %collective-permute-done.3.other_ref = bf16[16,2,32,128]{3,2,1,0:T(8,128)(2,1)S(1)} collective-permute-done((bf16[16,2,32,128]{3,2,1,0:T(8,128)(2,1)S(1)}, bf16[16,2,32,128]{3,2,1,0:T(8,128)(2,1)S(1)}, u32[]{:S(2)}, u32[]{:S(2)}) %collective-permute-start.3) | collective-permute-done | bytes 262176 | tf_op jit(solution)/shard_map/ppermute | solution.py:417
  15.3 0.6 mix_level.8.own_ref
  15.8 1.7 %collective-permute-start.4 = (bf16[16,2,32,128]{3,2,1,0:T(8,128)(2,1)S(1)}, bf16[16,2,32,128]{3,2,1,0:T(8,128)(2,1)}, u32[]{:S(2)}, u32[]{:S(2)}) collective-permute-start(bf16[16,2,32,128]{3,2,1,0:T(8,128)(2,1)S(1)} %mix_level.8.own_ref), channel_id=1, source_target_pairs={{0,32},{16,48},{32,0},{48,16},{64,96},{80,112},{96,64},{112,80},{1... | collective-permute-start | bytes 786440 | tf_op jit(solution)/shard_map/ppermute | solution.py:417
  17.6 0.7 copy-done.2
  18.3 0.9 %copy-done.1 = bf16[16,2,32,128]{3,2,1,0:T(8,128)(2,1)S(1)} copy-done((bf16[16,2,32,128]{3,2,1,0:T(8,128)(2,1)S(1)}, bf16[16,2,32,128]{3,2,1,0:T(8,128)(2,1)}, u32[]{:S(2)}) %copy-start.1) | copy-done | bytes 262168
  19.2 0.9 %copy-done.3 = bf16[16,2,32,128]{3,2,1,0:T(8,128)(2,1)S(1)} copy-done((bf16[16,2,32,128]{3,2,1,0:T(8,128)(2,1)S(1)}, bf16[16,2,32,128]{3,2,1,0:T(8,128)(2,1)}, u32[]{:S(2)}) %copy-start.3) | copy-done | bytes 262168
  20.2 2.2 %mix_level.6 = (bf16[16,2,32,128]{3,2,1,0:T(8,128)(2,1)}, bf16[16,2,2,64,128]{4,3,2,1,0:T(8,128)(2,1)S(1)}) custom-call(s32[1]{0:T(128)} %bitcast.3.upper_ref, bf16[16,2,32,128]{3,2,1,0:T(8,128)(2,1)S(1)} %copy-done.1, bf16[16,2,32,128]{3,2,1,0:T(8,128)(2,1)S(1)} %copy-done.3, bf16[16,4,2,64,128]{4,3,2,1,0:T(8,128)(2,1)S(1)} %get-tuple-element.14.factor_ref, ...), custom_call_target="tpu_custom_call" | custom-call | tf_op jit(solution)/shard_map/mix_level/pallas_call | solution.py:234
  22.3 0.4 collective-permute-start.1
  22.8 1.6 %collective-permute-done.4.other_ref = bf16[16,2,32,128]{3,2,1,0:T(8,128)(2,1)} collective-permute-done((bf16[16,2,32,128]{3,2,1,0:T(8,128)(2,1)S(1)}, bf16[16,2,32,128]{3,2,1,0:T(8,128)(2,1)}, u32[]{:S(2)}, u32[]{:S(2)}) %collective-permute-start.4) | collective-permute-done | bytes 262176 | tf_op jit(solution)/shard_map/ppermute | solution.py:417
  24.3 1.5 %mix_level.9.own_ref = bf16[16,2,32,128]{3,2,1,0:T(8,128)(2,1)S(1)} custom-call(s32[1]{0:T(128)} %bitcast.2.upper_ref, bf16[16,2,32,128]{3,2,1,0:T(8,128)(2,1)S(1)} %mix_level.8.own_ref, bf16[16,2,32,128]{3,2,1,0:T(8,128)(2,1)} %collective-permute-done.4.other_ref, bf16[16,2,2,64,128]{4,3,2,1,0:T(8,128)(2,1)S(1)} %get-tuple-element.17.factor_ref), custom_call_target="tpu_custom_call" | custom-call | tf_op jit(solution)/shard_map/mix_level/pallas_call | solution.py:234
  25.9 3.4 %collective-permute-start.5 = (bf16[16,2,32,128]{3,2,1,0:T(8,128)(2,1)S(1)}, bf16[16,2,32,128]{3,2,1,0:T(8,128)(2,1)S(1)}, u32[]{:S(2)}, u32[]{:S(2)}) collective-permute-start(bf16[16,2,32,128]{3,2,1,0:T(8,128)(2,1)S(1)} %mix_level.9.own_ref), channel_id=1, source_target_pairs={{0,64},{16,80},{32,96},{48,112},{64,0},{80,16},{96,32},{112,48},{1... | collective-permute-start | bytes 786440 | tf_op jit(solution)/shard_map/ppermute | solution.py:417
  29.2 2.3 %collective-permute-done.1.other_ref = bf16[16,2,32,128]{3,2,1,0:T(8,128)(2,1)S(1)} collective-permute-done((bf16[16,2,32,128]{3,2,1,0:T(8,128)(2,1)}, bf16[16,2,32,128]{3,2,1,0:T(8,128)(2,1)S(1)}, u32[]{:S(2)}, u32[]{:S(2)}) %collective-permute-start.1) | collective-permute-done | bytes 262176 | tf_op jit(solution)/shard_map/ppermute | solution.py:417
  31.6 2.8 %mix_level.7.own_ref = bf16[16,2,32,128]{3,2,1,0:T(8,128)(2,1)S(1)} custom-call(s32[1]{0:T(128)} %bitcast.2.upper_ref, bf16[16,2,32,128]{3,2,1,0:T(8,128)(2,1)} %get-tuple-element.15.own_ref, bf16[16,2,32,128]{3,2,1,0:T(8,128)(2,1)S(1)} %collective-permute-done.1.other_ref, bf16[3,16,4,2,64,128]{5,4,3,2,1,0:T(8,128)(2,1)} %bitcast.11), custom_call_target="tpu_custom_call" | custom-call | tf_op jit(solution)/shard_map/mix_level/pallas_call | solution.py:234
  34.4 3.2 %collective-permute-start.2 = (bf16[16,2,32,128]{3,2,1,0:T(8,128)(2,1)S(1)}, bf16[16,2,32,128]{3,2,1,0:T(8,128)(2,1)S(1)}, u32[]{:S(2)}, u32[]{:S(2)}) collective-permute-start(bf16[16,2,32,128]{3,2,1,0:T(8,128)(2,1)S(1)} %mix_level.7.own_ref), channel_id=1, source_target_pairs={{0,64},{16,80},{32,96},{48,112},{64,0},{80,16},{96,32},{112,48},{1... | collective-permute-start | bytes 786440 | tf_op jit(solution)/shard_map/ppermute | solution.py:417
  37.6 1.4 %collective-permute-done.5.other_ref = bf16[16,2,32,128]{3,2,1,0:T(8,128)(2,1)S(1)} collective-permute-done((bf16[16,2,32,128]{3,2,1,0:T(8,128)(2,1)S(1)}, bf16[16,2,32,128]{3,2,1,0:T(8,128)(2,1)S(1)}, u32[]{:S(2)}, u32[]{:S(2)}) %collective-permute-start.5) | collective-permute-done | bytes 262176 | tf_op jit(solution)/shard_map/ppermute | solution.py:417
  39.1 2.3 %mix_level.10 = (bf16[16,2,32,128]{3,2,1,0:T(8,128)(2,1)S(1)}, bf16[16,2,2,64,128]{4,3,2,1,0:T(8,128)(2,1)S(1)}, bf16[16,4,2,64,128]{4,3,2,1,0:T(8,128)(2,1)S(1)}) custom-call(s32[1]{0:T(128)} %bitcast.1.upper_ref, bf16[16,2,32,128]{3,2,1,0:T(8,128)(2,1)S(1)} %mix_level.9.own_ref, bf16[16,2,32,128]{3,2,1,0:T(8,128)(2,1)S(1)} %collective-permute-done.5.other_ref, ...), custom_call_target="tpu_custom_call" | custom-call | tf_op jit(solution)/shard_map/mix_level/pallas_call | solution.py:234
  41.3 2.3 %collective-permute-done.2.other_ref = bf16[16,2,32,128]{3,2,1,0:T(8,128)(2,1)S(1)} collective-permute-done((bf16[16,2,32,128]{3,2,1,0:T(8,128)(2,1)S(1)}, bf16[16,2,32,128]{3,2,1,0:T(8,128)(2,1)S(1)}, u32[]{:S(2)}, u32[]{:S(2)}) %collective-permute-start.2) | collective-permute-done | bytes 262176 | tf_op jit(solution)/shard_map/ppermute | solution.py:417
  43.6 0.6 mix_level.11
  44.2 18.0 %all_to_all.5.coef_ref = bf16[16,4,32,128]{3,2,1,0:T(8,128)(2,1)S(1)} all-to-all(bf16[16,4,32,128]{3,2,1,0:T(8,128)(2,1)S(1)} %mix_level.11), channel_id=1, replica_groups=mesh['lvl'=8,'clu'=16] {'clu'}, dimensions={0} | all-to-all | bytes 1048576 | tf_op jit(solution)/shard_map/all_to_all | solution.py:437
  62.2 18.2 %target_fields.1 = bf16[32,2,16384]{2,1,0:T(2,128)(2,1)} custom-call(s32[128,128]{1,0:T(8,128)} %bitcast.19, bf16[16,4,32,128]{3,2,1,0:T(8,128)(2,1)S(1)} %all_to_all.5.coef_ref, bf16[16,4,2,64,128]{4,3,2,1,0:T(8,128)(2,1)S(1)} %get-tuple-element.20.head, bf16[4,16,4,2,64,128]{5,4,3,2,1,0:T(8,128)(2,1)} %bitcast.15, bf16[16,4,64,512]{3,2,1,0:T(8,128)(2,1)} %bitcast.17), custom_call_target="tpu_custom_call" | custom-call | tf_op jit(solution)/shard_map/target_fields/pallas_call | solution.py:357
  (5 shorter events, 0.0 us)
Async XLA Ops:
  13.6 3.9 %copy-start = (bf16[16,2,32,128]{3,2,1,0:T(8,128)(2,1)}, bf16[16,2,32,128]{3,2,1,0:T(8,128)(2,1)S(1)}, u32[]{:S(2)}) copy-start(bf16[16,2,32,128]{3,2,1,0:T(8,128)(2,1)S(1)} %get-tuple-element.13.own_ref) | copy-start | bytes 786436
  13.6 1.6 %collective-permute-start.3 = (bf16[16,2,32,128]{3,2,1,0:T(8,128)(2,1)S(1)}, bf16[16,2,32,128]{3,2,1,0:T(8,128)(2,1)S(1)}, u32[]{:S(2)}, u32[]{:S(2)}) collective-permute-start(bf16[16,2,32,128]{3,2,1,0:T(8,128)(2,1)S(1)} %get-tuple-element.16.own_ref), channel_id=1, source_target_pairs={{0,16},{16,0},{32,48},{48,32},{64,80},{80,64},{96,112},{112,96},{1... | collective-permute-start | bytes 786440 | tf_op jit(solution)/shard_map/ppermute | solution.py:417
  13.7 3.8 %collective-permute-start = (bf16[16,2,32,128]{3,2,1,0:T(8,128)(2,1)S(1)}, bf16[16,2,32,128]{3,2,1,0:T(8,128)(2,1)S(1)}, u32[]{:S(2)}, u32[]{:S(2)}) collective-permute-start(bf16[16,2,32,128]{3,2,1,0:T(8,128)(2,1)S(1)} %get-tuple-element.13.own_ref), channel_id=1, source_target_pairs={{0,16},{16,0},{32,48},{48,32},{64,80},{80,64},{96,112},{112,96},{1... | collective-permute-start | bytes 786440 | tf_op jit(solution)/shard_map/ppermute | solution.py:417
  15.8 8.5 %collective-permute-start.4 = (bf16[16,2,32,128]{3,2,1,0:T(8,128)(2,1)S(1)}, bf16[16,2,32,128]{3,2,1,0:T(8,128)(2,1)}, u32[]{:S(2)}, u32[]{:S(2)}) collective-permute-start(bf16[16,2,32,128]{3,2,1,0:T(8,128)(2,1)S(1)} %mix_level.8.own_ref), channel_id=1, source_target_pairs={{0,32},{16,48},{32,0},{48,16},{64,96},{80,112},{96,64},{112,80},{1... | collective-permute-start | bytes 786440 | tf_op jit(solution)/shard_map/ppermute | solution.py:417
  17.6 0.7 copy-start.2
  18.3 0.9 %copy-start.1 = (bf16[16,2,32,128]{3,2,1,0:T(8,128)(2,1)S(1)}, bf16[16,2,32,128]{3,2,1,0:T(8,128)(2,1)}, u32[]{:S(2)}) copy-start(bf16[16,2,32,128]{3,2,1,0:T(8,128)(2,1)} %copy-done) | copy-start | bytes 786436
  19.2 0.9 %copy-start.3 = (bf16[16,2,32,128]{3,2,1,0:T(8,128)(2,1)S(1)}, bf16[16,2,32,128]{3,2,1,0:T(8,128)(2,1)}, u32[]{:S(2)}) copy-start(bf16[16,2,32,128]{3,2,1,0:T(8,128)(2,1)} %copy-done.2) | copy-start | bytes 786436
  22.3 9.2 %collective-permute-start.1 = (bf16[16,2,32,128]{3,2,1,0:T(8,128)(2,1)}, bf16[16,2,32,128]{3,2,1,0:T(8,128)(2,1)S(1)}, u32[]{:S(2)}, u32[]{:S(2)}) collective-permute-start(bf16[16,2,32,128]{3,2,1,0:T(8,128)(2,1)} %get-tuple-element.15.own_ref), channel_id=1, source_target_pairs={{0,32},{16,48},{32,0},{48,16},{64,96},{80,112},{96,64},{112,80},{1... | collective-permute-start | bytes 786440 | tf_op jit(solution)/shard_map/ppermute | solution.py:417
  25.9 13.2 %collective-permute-start.5 = (bf16[16,2,32,128]{3,2,1,0:T(8,128)(2,1)S(1)}, bf16[16,2,32,128]{3,2,1,0:T(8,128)(2,1)S(1)}, u32[]{:S(2)}, u32[]{:S(2)}) collective-permute-start(bf16[16,2,32,128]{3,2,1,0:T(8,128)(2,1)S(1)} %mix_level.9.own_ref), channel_id=1, source_target_pairs={{0,64},{16,80},{32,96},{48,112},{64,0},{80,16},{96,32},{112,48},{1... | collective-permute-start | bytes 786440 | tf_op jit(solution)/shard_map/ppermute | solution.py:417
  34.4 9.3 %collective-permute-start.2 = (bf16[16,2,32,128]{3,2,1,0:T(8,128)(2,1)S(1)}, bf16[16,2,32,128]{3,2,1,0:T(8,128)(2,1)S(1)}, u32[]{:S(2)}, u32[]{:S(2)}) collective-permute-start(bf16[16,2,32,128]{3,2,1,0:T(8,128)(2,1)S(1)} %mix_level.7.own_ref), channel_id=1, source_target_pairs={{0,64},{16,80},{32,96},{48,112},{64,0},{80,16},{96,32},{112,48},{1... | collective-permute-start | bytes 786440 | tf_op jit(solution)/shard_map/ppermute | solution.py:417

commit v5 on v3

--- a/solution.py
+++ b/solution.py
@@ -240,7 +240,7 @@
         + [ANYWHERE] * len(ahead),
         out_specs=[VMEM] * (1 + len(ahead)),
         scratch_shapes=scratch + [pltpu.SemaphoreType.DMA((2 + len(ahead),))],
-        compiler_params=pltpu.CompilerParams(vmem_limit_bytes=6 << 20),
+        compiler_params=pltpu.CompilerParams(vmem_limit_bytes=3 << 20),
         name="mix_level",
     )(
         upper, own, other, in_vmem(factors) if resident else in_hbm(factors),

time: 81.3 us -> 81.3 us (level)
  no operation moved by 1% of the time
where the time goes in v5:
time: 81.3 us; the launch traced here: 81 us
  Pallas kernels  42.1 us (52%)
  blocking collectives  18 us (22%)
  starting transfers between devices  9.37 us (12%)
  waiting for transfers between devices  8.66 us (11%)
  local copies, waits for them, and re-layouts  2.62 us (3%)
    pallas_call x1, Pallas kernels, target_fields(): pl.pallas_call(target_kernel, out_shape=jax.ShapeDtypeStruct((rhs, 2, blo...  18.5 us
    all_to_all x1, blocking collectives, local(): lax.all_to_all(coefs[-1], 'clu', split_axis=0, concat_axis=0, tiled=True)  18 us
    pallas_call x1, Pallas kernels, leaf_coefs(): pl.pallas_call(leaf_kernel, out_shape=[coef] * PARTS + [pltpu.VMEM(x.shap...  13.8 us
    pallas_call x6, Pallas kernels, mix_level(): pl.pallas_call(functools.partial(mix_kernel, level, first, resident, len(...  9.85 us
    ppermute x6, starting transfers between devices, local(): other = lax.ppermute(coefs[k], 'lvl', swap)  9.37 us
    ppermute x6, waiting for transfers between devices, local(): other = lax.ppermute(coefs[k], 'lvl', swap)  8.66 us
    unnamed x8, local copies, waits for them, and re-layouts  2.62 us
  transfers between devices with their start and end apart: 6, of which 5 were waited for; matrix products, arithmetic and copies ran while one was open for 0% of the time, Pallas kernels for 11%

profile of v5, /device:TPU:0, one launch (start us, length us, event | category | flops | bytes accessed | tf_op | source)
XLA Modules:
  0.0 81.0 jit_solution(5368182864181123515)
XLA Ops:
  0.0 13.8 %leaf_coefs.1 = (bf16[16,2,32,128]{3,2,1,0:T(8,128)(2,1)S(1)}, bf16[16,2,32,128]{3,2,1,0:T(8,128)(2,1)S(1)}, bf16[16,4,2,64,128]{4,3,2,1,0:T(8,128)(2,1)S(1)}) custom-call(s32[128,128]{1,0:T(8,128)} %bitcast.18, s32[64]{0:T(128)} %ranks_hbm.1, bf16[32,2,16384]{2,1,0:T(2,128)(2,1)} %source_hbm.1, bf16[16,4,256,128]{3,2,1,0:T(8,128)(2,1)} %bitcast.16, ...), custom_call_target="tpu_custom_call" | custom-call | tf_op jit(solution)/shard_map/leaf_coefs/pallas_call | solution.py:158
  13.8 0.0 copy-start
  13.8 0.1 collective-permute-start.3
  13.9 0.5 collective-permute-start
  14.4 1.0 %collective-permute-done.3.other_ref = bf16[16,2,32,128]{3,2,1,0:T(8,128)(2,1)S(1)} collective-permute-done((bf16[16,2,32,128]{3,2,1,0:T(8,128)(2,1)S(1)}, bf16[16,2,32,128]{3,2,1,0:T(8,128)(2,1)S(1)}, u32[]{:S(2)}, u32[]{:S(2)}) %collective-permute-start.3) | collective-permute-done | bytes 262176 | tf_op jit(solution)/shard_map/ppermute | solution.py:417
  15.5 0.6 mix_level.8.own_ref
  16.0 1.7 %collective-permute-start.4 = (bf16[16,2,32,128]{3,2,1,0:T(8,128)(2,1)S(1)}, bf16[16,2,32,128]{3,2,1,0:T(8,128)(2,1)}, u32[]{:S(2)}, u32[]{:S(2)}) collective-permute-start(bf16[16,2,32,128]{3,2,1,0:T(8,128)(2,1)S(1)} %mix_level.8.own_ref), channel_id=1, source_target_pairs={{0,32},{16,48},{32,0},{48,16},{64,96},{80,112},{96,64},{112,80},{1... | collective-permute-start | bytes 786440 | tf_op jit(solution)/shard_map/ppermute | solution.py:417
  17.8 0.7 copy-done.2
  18.5 0.9 %copy-done.1 = bf16[16,2,32,128]{3,2,1,0:T(8,128)(2,1)S(1)} copy-done((bf16[16,2,32,128]{3,2,1,0:T(8,128)(2,1)S(1)}, bf16[16,2,32,128]{3,2,1,0:T(8,128)(2,1)}, u32[]{:S(2)}) %copy-start.1) | copy-done | bytes 262168
  19.4 0.9 %copy-done.3 = bf16[16,2,32,128]{3,2,1,0:T(8,128)(2,1)S(1)} copy-done((bf16[16,2,32,128]{3,2,1,0:T(8,128)(2,1)S(1)}, bf16[16,2,32,128]{3,2,1,0:T(8,128)(2,1)}, u32[]{:S(2)}) %copy-start.3) | copy-done | bytes 262168
  20.4 2.2 %mix_level.6 = (bf16[16,2,32,128]{3,2,1,0:T(8,128)(2,1)}, bf16[16,2,2,64,128]{4,3,2,1,0:T(8,128)(2,1)S(1)}) custom-call(s32[1]{0:T(128)} %bitcast.3.upper_ref, bf16[16,2,32,128]{3,2,1,0:T(8,128)(2,1)S(1)} %copy-done.1, bf16[16,2,32,128]{3,2,1,0:T(8,128)(2,1)S(1)} %copy-done.3, bf16[16,4,2,64,128]{4,3,2,1,0:T(8,128)(2,1)S(1)} %get-tuple-element.14.factor_ref, ...), custom_call_target="tpu_custom_call" | custom-call | tf_op jit(solution)/shard_map/mix_level/pallas_call | solution.py:234
  22.6 0.4 collective-permute-start.1
  23.0 1.6 %collective-permute-done.4.other_ref = bf16[16,2,32,128]{3,2,1,0:T(8,128)(2,1)} collective-permute-done((bf16[16,2,32,128]{3,2,1,0:T(8,128)(2,1)S(1)}, bf16[16,2,32,128]{3,2,1,0:T(8,128)(2,1)}, u32[]{:S(2)}, u32[]{:S(2)}) %collective-permute-start.4) | collective-permute-done | bytes 262176 | tf_op jit(solution)/shard_map/ppermute | solution.py:417
  24.6 1.5 %mix_level.9.own_ref = bf16[16,2,32,128]{3,2,1,0:T(8,128)(2,1)S(1)} custom-call(s32[1]{0:T(128)} %bitcast.2.upper_ref, bf16[16,2,32,128]{3,2,1,0:T(8,128)(2,1)S(1)} %mix_level.8.own_ref, bf16[16,2,32,128]{3,2,1,0:T(8,128)(2,1)} %collective-permute-done.4.other_ref, bf16[16,2,2,64,128]{4,3,2,1,0:T(8,128)(2,1)S(1)} %get-tuple-element.17.factor_ref), custom_call_target="tpu_custom_call" | custom-call | tf_op jit(solution)/shard_map/mix_level/pallas_call | solution.py:234
  26.1 3.4 %collective-permute-start.5 = (bf16[16,2,32,128]{3,2,1,0:T(8,128)(2,1)S(1)}, bf16[16,2,32,128]{3,2,1,0:T(8,128)(2,1)S(1)}, u32[]{:S(2)}, u32[]{:S(2)}) collective-permute-start(bf16[16,2,32,128]{3,2,1,0:T(8,128)(2,1)S(1)} %mix_level.9.own_ref), channel_id=1, source_target_pairs={{0,64},{16,80},{32,96},{48,112},{64,0},{80,16},{96,32},{112,48},{1... | collective-permute-start | bytes 786440 | tf_op jit(solution)/shard_map/ppermute | solution.py:417
  29.4 2.3 %collective-permute-done.1.other_ref = bf16[16,2,32,128]{3,2,1,0:T(8,128)(2,1)S(1)} collective-permute-done((bf16[16,2,32,128]{3,2,1,0:T(8,128)(2,1)}, bf16[16,2,32,128]{3,2,1,0:T(8,128)(2,1)S(1)}, u32[]{:S(2)}, u32[]{:S(2)}) %collective-permute-start.1) | collective-permute-done | bytes 262176 | tf_op jit(solution)/shard_map/ppermute | solution.py:417
  31.8 2.8 %mix_level.7.own_ref = bf16[16,2,32,128]{3,2,1,0:T(8,128)(2,1)S(1)} custom-call(s32[1]{0:T(128)} %bitcast.2.upper_ref, bf16[16,2,32,128]{3,2,1,0:T(8,128)(2,1)} %get-tuple-element.15.own_ref, bf16[16,2,32,128]{3,2,1,0:T(8,128)(2,1)S(1)} %collective-permute-done.1.other_ref, bf16[3,16,4,2,64,128]{5,4,3,2,1,0:T(8,128)(2,1)} %bitcast.11), custom_call_target="tpu_custom_call" | custom-call | tf_op jit(solution)/shard_map/mix_level/pallas_call | solution.py:234
  34.6 3.2 %collective-permute-start.2 = (bf16[16,2,32,128]{3,2,1,0:T(8,128)(2,1)S(1)}, bf16[16,2,32,128]{3,2,1,0:T(8,128)(2,1)S(1)}, u32[]{:S(2)}, u32[]{:S(2)}) collective-permute-start(bf16[16,2,32,128]{3,2,1,0:T(8,128)(2,1)S(1)} %mix_level.7.own_ref), channel_id=1, source_target_pairs={{0,64},{16,80},{32,96},{48,112},{64,0},{80,16},{96,32},{112,48},{1... | collective-permute-start | bytes 786440 | tf_op jit(solution)/shard_map/ppermute | solution.py:417
  37.8 1.4 %collective-permute-done.5.other_ref = bf16[16,2,32,128]{3,2,1,0:T(8,128)(2,1)S(1)} collective-permute-done((bf16[16,2,32,128]{3,2,1,0:T(8,128)(2,1)S(1)}, bf16[16,2,32,128]{3,2,1,0:T(8,128)(2,1)S(1)}, u32[]{:S(2)}, u32[]{:S(2)}) %collective-permute-start.5) | collective-permute-done | bytes 262176 | tf_op jit(solution)/shard_map/ppermute | solution.py:417
  39.3 2.3 %mix_level.10 = (bf16[16,2,32,128]{3,2,1,0:T(8,128)(2,1)S(1)}, bf16[16,2,2,64,128]{4,3,2,1,0:T(8,128)(2,1)S(1)}, bf16[16,4,2,64,128]{4,3,2,1,0:T(8,128)(2,1)S(1)}) custom-call(s32[1]{0:T(128)} %bitcast.1.upper_ref, bf16[16,2,32,128]{3,2,1,0:T(8,128)(2,1)S(1)} %mix_level.9.own_ref, bf16[16,2,32,128]{3,2,1,0:T(8,128)(2,1)S(1)} %collective-permute-done.5.other_ref, ...), custom_call_target="tpu_custom_call" | custom-call | tf_op jit(solution)/shard_map/mix_level/pallas_call | solution.py:234
  41.5 2.3 %collective-permute-done.2.other_ref = bf16[16,2,32,128]{3,2,1,0:T(8,128)(2,1)S(1)} collective-permute-done((bf16[16,2,32,128]{3,2,1,0:T(8,128)(2,1)S(1)}, bf16[16,2,32,128]{3,2,1,0:T(8,128)(2,1)S(1)}, u32[]{:S(2)}, u32[]{:S(2)}) %collective-permute-start.2) | collective-permute-done | bytes 262176 | tf_op jit(solution)/shard_map/ppermute | solution.py:417
  43.8 0.6 mix_level.11
  44.4 18.0 %all_to_all.5.coef_ref = bf16[16,4,32,128]{3,2,1,0:T(8,128)(2,1)S(1)} all-to-all(bf16[16,4,32,128]{3,2,1,0:T(8,128)(2,1)S(1)} %mix_level.11), channel_id=1, replica_groups=mesh['lvl'=8,'clu'=16] {'clu'}, dimensions={0} | all-to-all | bytes 1048576 | tf_op jit(solution)/shard_map/all_to_all | solution.py:437
  62.4 18.5 %target_fields.1 = bf16[32,2,16384]{2,1,0:T(2,128)(2,1)} custom-call(s32[128,128]{1,0:T(8,128)} %bitcast.19, bf16[16,4,32,128]{3,2,1,0:T(8,128)(2,1)S(1)} %all_to_all.5.coef_ref, bf16[16,4,2,64,128]{4,3,2,1,0:T(8,128)(2,1)S(1)} %get-tuple-element.20.head, bf16[4,16,4,2,64,128]{5,4,3,2,1,0:T(8,128)(2,1)} %bitcast.15, bf16[16,4,64,512]{3,2,1,0:T(8,128)(2,1)} %bitcast.17), custom_call_target="tpu_custom_call" | custom-call | tf_op jit(solution)/shard_map/target_fields/pallas_call | solution.py:357
  (5 shorter events, 0.0 us)
Async XLA Ops:
  13.8 3.9 %copy-start = (bf16[16,2,32,128]{3,2,1,0:T(8,128)(2,1)}, bf16[16,2,32,128]{3,2,1,0:T(8,128)(2,1)S(1)}, u32[]{:S(2)}) copy-start(bf16[16,2,32,128]{3,2,1,0:T(8,128)(2,1)S(1)} %get-tuple-element.13.own_ref) | copy-start | bytes 786436
  13.8 1.6 %collective-permute-start.3 = (bf16[16,2,32,128]{3,2,1,0:T(8,128)(2,1)S(1)}, bf16[16,2,32,128]{3,2,1,0:T(8,128)(2,1)S(1)}, u32[]{:S(2)}, u32[]{:S(2)}) collective-permute-start(bf16[16,2,32,128]{3,2,1,0:T(8,128)(2,1)S(1)} %get-tuple-element.16.own_ref), channel_id=1, source_target_pairs={{0,16},{16,0},{32,48},{48,32},{64,80},{80,64},{96,112},{112,96},{1... | collective-permute-start | bytes 786440 | tf_op jit(solution)/shard_map/ppermute | solution.py:417
  13.9 3.8 %collective-permute-start = (bf16[16,2,32,128]{3,2,1,0:T(8,128)(2,1)S(1)}, bf16[16,2,32,128]{3,2,1,0:T(8,128)(2,1)S(1)}, u32[]{:S(2)}, u32[]{:S(2)}) collective-permute-start(bf16[16,2,32,128]{3,2,1,0:T(8,128)(2,1)S(1)} %get-tuple-element.13.own_ref), channel_id=1, source_target_pairs={{0,16},{16,0},{32,48},{48,32},{64,80},{80,64},{96,112},{112,96},{1... | collective-permute-start | bytes 786440 | tf_op jit(solution)/shard_map/ppermute | solution.py:417
  16.0 8.5 %collective-permute-start.4 = (bf16[16,2,32,128]{3,2,1,0:T(8,128)(2,1)S(1)}, bf16[16,2,32,128]{3,2,1,0:T(8,128)(2,1)}, u32[]{:S(2)}, u32[]{:S(2)}) collective-permute-start(bf16[16,2,32,128]{3,2,1,0:T(8,128)(2,1)S(1)} %mix_level.8.own_ref), channel_id=1, source_target_pairs={{0,32},{16,48},{32,0},{48,16},{64,96},{80,112},{96,64},{112,80},{1... | collective-permute-start | bytes 786440 | tf_op jit(solution)/shard_map/ppermute | solution.py:417
  17.8 0.7 copy-start.2
  18.5 0.9 %copy-start.1 = (bf16[16,2,32,128]{3,2,1,0:T(8,128)(2,1)S(1)}, bf16[16,2,32,128]{3,2,1,0:T(8,128)(2,1)}, u32[]{:S(2)}) copy-start(bf16[16,2,32,128]{3,2,1,0:T(8,128)(2,1)} %copy-done) | copy-start | bytes 786436
  19.4 0.9 %copy-start.3 = (bf16[16,2,32,128]{3,2,1,0:T(8,128)(2,1)S(1)}, bf16[16,2,32,128]{3,2,1,0:T(8,128)(2,1)}, u32[]{:S(2)}) copy-start(bf16[16,2,32,128]{3,2,1,0:T(8,128)(2,1)} %copy-done.2) | copy-start | bytes 786436
  22.6 9.2 %collective-permute-start.1 = (bf16[16,2,32,128]{3,2,1,0:T(8,128)(2,1)}, bf16[16,2,32,128]{3,2,1,0:T(8,128)(2,1)S(1)}, u32[]{:S(2)}, u32[]{:S(2)}) collective-permute-start(bf16[16,2,32,128]{3,2,1,0:T(8,128)(2,1)} %get-tuple-element.15.own_ref), channel_id=1, source_target_pairs={{0,32},{16,48},{32,0},{48,16},{64,96},{80,112},{96,64},{112,80},{1... | collective-permute-start | bytes 786440 | tf_op jit(solution)/shard_map/ppermute | solution.py:417
  26.1 13.2 %collective-permute-start.5 = (bf16[16,2,32,128]{3,2,1,0:T(8,128)(2,1)S(1)}, bf16[16,2,32,128]{3,2,1,0:T(8,128)(2,1)S(1)}, u32[]{:S(2)}, u32[]{:S(2)}) collective-permute-start(bf16[16,2,32,128]{3,2,1,0:T(8,128)(2,1)S(1)} %mix_level.9.own_ref), channel_id=1, source_target_pairs={{0,64},{16,80},{32,96},{48,112},{64,0},{80,16},{96,32},{112,48},{1... | collective-permute-start | bytes 786440 | tf_op jit(solution)/shard_map/ppermute | solution.py:417
  34.6 9.3 %collective-permute-start.2 = (bf16[16,2,32,128]{3,2,1,0:T(8,128)(2,1)S(1)}, bf16[16,2,32,128]{3,2,1,0:T(8,128)(2,1)S(1)}, u32[]{:S(2)}, u32[]{:S(2)}) collective-permute-start(bf16[16,2,32,128]{3,2,1,0:T(8,128)(2,1)S(1)} %mix_level.7.own_ref), channel_id=1, source_target_pairs={{0,64},{16,80},{32,96},{48,112},{64,0},{80,16},{96,32},{112,48},{1... | collective-permute-start | bytes 786440 | tf_op jit(solution)/shard_map/ppermute | solution.py:417
